TPU v7x, 128 devices: a whole 4x4x4 slice. The times are simulated.
128 devices in a mesh: chan: 16 (over x_lo, z, core), seg: 8 (over y, x_hi).
Axes of the slice: x: 4 (x_hi: 2, x_lo: 2; x = x_hi * 2 + x_lo), y: 4, z: 4, core: 2. Of those that a mesh axis runs over, the one named last changes fastest.
Arguments:
- strain_rate: bfloat16 [1536, 270336], P('chan', 'seg'), may hold values from -56 to 56
- window_starts: int32 [512], P('seg'), may hold values from 0 to 128
Outputs:
- cross_spectra: float32 [96, 2, 1536, 1536], P('seg', None, 'chan')
All inputs are finite; a program needn't handle non-finite values.
Results may differ from a plain program's by a relative error of at most 0.00096.
Values may be sent and summed in bfloat16 or wider, within the bound.
No kernel may reach another device: no remote copies, remote signals or barrier semaphores. Data moves between devices by JAX's collectives and lax.ppermute only.
A program may use at most 192 MiB of HBM per device.

v0:
```python
import math

import jax
import jax.numpy as jnp
from jax import lax
from jax.sharding import PartitionSpec as P

WIN = 1024
F = 96
K0 = 10


EPSILON = 1e-06
CLIP_LEVEL = 1.5


def paired_table(length, first_bin, bin_count):
    sample_ids = jnp.arange(length, dtype=jnp.int32)
    bin_ids = first_bin + jnp.arange(bin_count, dtype=jnp.int32)
    phase_turns = (bin_ids[:, None] * sample_ids[None, :] % length).astype(jnp.float32) * (
        2.0 * math.pi / length
    )
    paired = jnp.stack([jnp.cos(phase_turns), -jnp.sin(phase_turns)], 1)
    return paired.reshape(2 * bin_count, length).astype(jnp.bfloat16)


def local_spectra(samples, starts, table):
    length = table.shape[1]
    quarter = length // 4
    channels = samples.shape[0]
    window_count = starts.shape[0]
    blocks = samples.reshape(channels, samples.shape[1] // quarter, quarter)
    block_index = starts[:, None] + jnp.arange(4, dtype=jnp.int32)[None, :]
    windows = (
        jnp.take(blocks, block_index, axis=1)
        .reshape(channels, window_count, length)
        .astype(jnp.float32)
    )
    spread = jnp.sqrt(jnp.mean(windows * windows, -1, keepdims=True) + EPSILON)
    hann_window = 0.5 - 0.5 * jnp.cos(
        jnp.arange(length, dtype=jnp.float32) * (2.0 * math.pi / length)
    )
    tapered = (jnp.clip(windows, -CLIP_LEVEL * spread, CLIP_LEVEL * spread) * hann_window).astype(
        jnp.bfloat16
    )
    spectrum = lax.dot_general(
        table, tapered, (((1,), (2,)), ((), ())), preferred_element_type=jnp.float32
    )
    band_power = jnp.mean(spectrum * spectrum, 0, keepdims=True) + EPSILON
    whitened = (spectrum / jnp.sqrt(band_power)).astype(jnp.bfloat16)
    whitened = whitened.reshape(table.shape[0] // 2, 2, channels, window_count)
    return jnp.swapaxes(whitened, 1, 2)


def augmented_rows(operand):
    real_rows = operand[:, :, 0, :]
    imag_rows = operand[:, :, 1, :]
    upper = jnp.concatenate([real_rows, imag_rows], 2)
    lower = jnp.concatenate([imag_rows, -real_rows], 2)
    return jnp.concatenate([upper, lower], 1)


def cross_tile(augmented, partner):
    flat = partner.reshape(partner.shape[0], partner.shape[1], partner.shape[2] * partner.shape[3])
    products = lax.dot_general(
        augmented, flat, (((2,), (2,)), ((0,), (0,))), preferred_element_type=jnp.float32
    )
    return products.reshape(products.shape[0], 2, products.shape[1] // 2, products.shape[2])


def local(strain_rate, window_starts):
    table = paired_table(WIN, K0, F)
    spectra = local_spectra(strain_rate, window_starts, table)
    segments = lax.axis_size("seg")
    operand = lax.all_to_all(spectra, "seg", split_axis=0, concat_axis=3, tiled=True)
    augmented = augmented_rows(operand)
    stacked = cross_tile(augmented, lax.all_gather(operand, "chan", axis=1, tiled=True))
    return stacked / (segments * spectra.shape[3])


def solution(mesh):
    in_specs = (P("chan", "seg"), P("seg"))
    out_specs = P("seg", None, "chan", None)
    return jax.shard_map(local, mesh=mesh, in_specs=in_specs, out_specs=out_specs, check_vma=False)
```

profile of v0, /device:TPU:1, one launch (start us, length us, event | category | flops | bytes accessed | tf_op | source)
XLA Modules:
  0.0 428.5 jit_solution(14664398078783628219)
XLA Ops:
  6.5 0.0 all-gather.2.cloned.1.call-start
  6.5 0.1 multiply_subtract_fusion
  6.6 0.7 fusion.22
  7.3 0.7 compare_select_fusion
  8.0 0.1 copy.36
  8.1 0.1 reshape.244
  8.2 1.8 cosine_convert_fusion
  10.1 0.4 copy.35
  10.5 0.1 reshape.251
  10.7 6.5 %copy.51 = bf16[12,132,8,256]{3,2,0,1:T(8,128)(2,1)} copy(bf16[12,132,8,256]{3,2,1,0:T(8,128)(2,1)} %bitcast.47) | data formatting | bytes 12976128 | tf_op jit(solution)/shard_map/reshape | solution.py:32
  17.2 13.7 %gather_fusion = bf16[256,96,256]{2,1,0:T(8,128)(2,1)} fusion(bf16[96,132,256]{2,0,1:T(8,128)(2,1)} %bitcast.40, s32[1024]{0:T(1024)S(1)} %pad_clamp_fusion), kind=kCustom, calls=%fused_computation | custom fusion | bytes 25166848 | tf_op jit(solution)/shard_map/jit(_take)/gather | solution.py:35
  30.8 8.2 %fusion = f32[96,64]{0,1:T(8,128)S(1)} fusion(bf16[64,4,96,256]{3,2,1,0:T(8,128)(2,1)} %bitcast.39, pred[64,4]{1,0:T(8,128)(4,1)S(1)} %copy.36), kind=kLoop, calls=%fused_computation.3 | loop fusion | flops 25159680 | bytes 12607744 | tf_op jit(solution)/shard_map/reduce_sum | solution.py:39
  39.1 16.6 %fusion.4 = bf16[64,4,12,8,256]{4,3,2,1,0:T(8,128)(2,1)S(1)} fusion(f32[4,256]{1,0:T(4,128)S(1)} %multiply_subtract_fusion, f32[96,64]{0,1:T(8,128)S(1)} %get-tuple-element.8, f32[96,64]{0,1:T(8,128)S(1)} %get-tuple-element.7, pred[64,4]{1,0:T(8,128)(4,1)S(1)} %copy.36, bf16[256,96,256]{2,1,0:T(8,128)(2,1)} %gather_fusion), kind=kLoop, calls=%fused_computation.7 | loop fusion | flops 37748736 | bytes 25219328
  55.7 2.0 copy.48
  57.7 4.6 %multiply_reduce_fusion = (f32[96,64]{0,1:T(8,128)S(1)}, f32[192,96,64]{1,0,2:T(8,128)S(1)}) fusion(bf16[192,1024,1]{1,0,2:T(8,128)(2,1)S(1)} %reshape.251, bf16[96,64,1024]{2,0,1:T(8,128)(2,1)S(1)} %bitcast.43), kind=kOutput, calls=%fused_computation.12 | convolution fusion | flops 2418272256 | bytes 17719296 | tf_op jit(solution)/shard_map/dot_general | solution.py:46
  62.3 0.9 divide_convert_fusion
  63.3 3.6 copy.52
  66.9 46.0 %all_to_all.18 = bf16[96,96,2,64]{1,3,2,0:T(8,128)(2,1)S(1)} all-to-all(bf16[96,96,2,64]{1,3,2,0:T(8,128)(2,1)S(1)} %bitcast.44), channel_id=1, replica_groups=mesh['chan'=16,'seg'=8] {'seg'}, dimensions={0} | all-to-all | bytes 4718592 | tf_op jit(solution)/shard_map/all_to_all | solution.py:75
  113.0 0.9 copy.40
  113.9 3.9 copy.43
  117.9 0.0 all-gather.2.cloned.1.call-update
  117.9 1.8 fusion.24
  119.7 1.7 copy.46
  121.4 1.7 copy.45
  123.1 0.1 bitcast_negate_fusion
  123.2 185.2 %all-gather.2.cloned.1.call-done = bf16[12,1536,2,512]{3,2,0,1:T(2,128)(2,1)} async-done(((bf16[12,96,2,512]{3,2,0,1:T(2,128)(2,1)}), bf16[12,1536,2,512]{3,2,0,1:T(2,128)(2,1)}) %all-gather.2.cloned.1.call-update) | async-done | bytes 37748752 | tf_op jit(solution)/shard_map/all_gather | solution.py:77
  308.4 29.8 %copy.44 = bf16[12,1536,2,512]{3,2,1,0:T(2,128)(2,1)} copy(bf16[12,1536,2,512]{3,2,0,1:T(2,128)(2,1)} %all-gather.2.cloned.1.call-done) | data formatting | bytes 75497472 | tf_op jit(solution)/shard_map/all_gather | solution.py:77
  338.2 60.2 %reshape.241 = bf16[12,1536,1024]{2,1,0:T(8,128)(2,1)} reshape(bf16[12,1536,2,512]{3,2,1,0:T(2,128)(2,1)} %copy.44) | data formatting | bytes 75497472 | tf_op jit(solution)/shard_map/reshape | solution.py:64
  398.4 23.3 %broadcast_multiply_fusion = f32[12,192,1536]{2,1,0:T(8,128)} fusion(bf16[12,1536,1024]{2,1,0:T(8,128)(2,1)} %reshape.241, bf16[12,96,512]{2,1,0:T(8,128)(2,1)S(1)} %bitcast_negate_fusion, bf16[12,96,512]{2,1,0:T(8,128)(2,1)S(1)} %bitcast.49, bf16[12,96,512]{2,1,0:T(8,128)(2,1)S(1)} %bitcast.48), kind=kOutput, calls=%fused_computation.9 | convolution fusion | flops 7270170624 | bytes 55443456 | tf_op jit(solution)/shard_map/dot_general | solution.py:65
  (5 shorter events, 0.1 us)
Async XLA Ops:
  6.5 301.8 %all-gather.2.cloned.1.call-start = ((), (), s32[]{:S(2)}) async-start(), calls=%async_computation.1 | async-start | bytes 40108032 | tf_op jit(solution)/shard_map/all_gather | solution.py:77
Sparse Core Ops, SparseCore 0:
  118.0 190.3 all-gather.1
where the time goes:
time: 430 us; the launch traced here: 428 us
  waiting for transfers between devices  185 us (43%)
  local copies, waits for them, and re-layouts  127 us (30%)
  blocking collectives  46 us (11%)
  other arithmetic  29.2 us (7%)
  matrix products  27.9 us (6%)
  between operations  13.5 us (3%)
    all_gather x1, waiting for transfers between devices, local(): lax.all_gather(operand, 'chan', axis=1, tiled=True)  185 us
    reshape x1, local copies, waits for them, and re-layouts, cross_tile(): partner.reshape(partner.shape[0], partner.shape[1], partner.shape[2] * pa...  60.2 us
    all_to_all x1, blocking collectives, local(): lax.all_to_all(spectra, 'seg', split_axis=0, concat_axis=3, tiled=True)  46 us
    all_gather x1, local copies, waits for them, and re-layouts, local(): lax.all_gather(operand, 'chan', axis=1, tiled=True)  29.8 us
    dot_general x1, matrix products, cross_tile(): lax.dot_general(augmented, flat, (((2,), (2,)), ((0,), (0,))), preferred_...  23.3 us
    unnamed x1, other arithmetic  16.6 us
    gather x1, local copies, waits for them, and re-layouts, local_spectra(): jnp.take(blocks, block_index, axis=1)  13.7 us
  transfers between devices with their start and end apart: 1, of which 1 were waited for; matrix products, arithmetic and copies ran while one was open for 1% of the time, Pallas kernels for 0%

commit v1 on v0

v1 whole, which is shorter than its diff:
```python
import functools
import math

import jax
import jax.numpy as jnp
import numpy as np
from jax import lax
from jax.experimental import pallas as pl
from jax.experimental.pallas import tpu as pltpu
from jax.sharding import PartitionSpec as P
import ml_dtypes

WIN = 1024
QUARTER = WIN // 4
F = 96
K0 = 10
EPSILON = 1e-06
CLIP_LEVEL = 1.5
LANES = 128
GROUP = 32


def fourier_columns():
    n = np.arange(WIN, dtype=np.int64)
    k = K0 + np.arange(F, dtype=np.int64)
    m = (n[:, None] * k[None, :]) % WIN
    phase = (m.astype(np.float32) * np.float32(2.0 * math.pi / WIN)).astype(np.float64)
    table = np.zeros((WIN, 2 * LANES), np.float32)
    table[:, :F] = np.cos(phase)
    table[:, LANES : LANES + F] = -np.sin(phase)
    return table.astype(ml_dtypes.bfloat16)


def hann_row():
    phase = (np.arange(WIN, dtype=np.float32) * np.float32(2.0 * math.pi / WIN)).astype(np.float64)
    return (0.5 - 0.5 * np.cos(phase)).astype(np.float32)[None, :]


def spectra_kernel(starts, samples, table, hann, out, taps, real, imag, staged):
    group = samples.shape[0]
    windows = starts.shape[0]

    def one_window(w, _):
        first = pl.multiple_of(starts[w] * QUARTER, QUARTER)
        win = samples[:, pl.ds(first, WIN)].astype(jnp.float32)
        power = jnp.sum(win * win, -1, keepdims=True) * (1.0 / WIN)
        level = CLIP_LEVEL * jnp.sqrt(power + EPSILON)
        tap = jnp.clip(win, -level, level) * hann[...]
        taps[pl.ds(pl.multiple_of(w * group, group), group), :] = tap.astype(jnp.bfloat16)
        return 0

    lax.fori_loop(0, windows, one_window, 0, unroll=2)

    rows = 512

    def one_dot(i, _):
        at = pl.ds(pl.multiple_of(i * rows, rows), rows)
        spec = jnp.dot(taps[at, :], table[...], preferred_element_type=jnp.float32)
        real[at, :] = spec[:, :LANES]
        imag[at, :] = spec[:, LANES:]
        return 0

    lax.fori_loop(0, windows * group // rows, one_dot, 0)

    def one_channel(c, _):
        at = pl.ds(c, windows, stride=group)
        both = jnp.concatenate([real[at, :], imag[at, :]], 0)
        turned = both.T[:F]
        total = jnp.sum(turned * turned, 0, keepdims=True)
        total = total + pltpu.roll(total, windows, 1)
        scale = lax.rsqrt(total * (1.0 / (2 * F)) + EPSILON)
        staged[pl.ds(c, F, stride=group), :] = turned * scale
        return 0

    lax.fori_loop(0, group, one_channel, 0, unroll=2)
    out[...] = staged[...].reshape(F, group, LANES).astype(jnp.bfloat16)


def local_spectra(samples, starts):
    channels, length = samples.shape
    windows = starts.shape[0]
    return pl.pallas_call(
        spectra_kernel,
        grid=(channels // GROUP,),
        in_specs=[
            pl.BlockSpec(memory_space=pltpu.SMEM),
            pl.BlockSpec((GROUP, length), lambda g: (g, 0)),
            pl.BlockSpec((WIN, 2 * LANES), lambda g: (0, 0)),
            pl.BlockSpec((1, WIN), lambda g: (0, 0)),
        ],
        out_specs=pl.BlockSpec((F, GROUP, LANES), lambda g: (0, g, 0)),
        out_shape=jax.ShapeDtypeStruct((F, channels, LANES), jnp.bfloat16),
        scratch_shapes=[
            pltpu.VMEM((windows * GROUP, WIN), jnp.bfloat16),
            pltpu.VMEM((windows * GROUP, LANES), jnp.float32),
            pltpu.VMEM((windows * GROUP, LANES), jnp.float32),
            pltpu.VMEM((F * GROUP, LANES), jnp.float32),
        ],
        compiler_params=pltpu.CompilerParams(vmem_limit_bytes=48 * 1024 * 1024),
        name="spectra",
    )(starts, samples, jnp.asarray(fourier_columns()), jnp.asarray(hann_row()))


def merge_kernel(parts, out):
    out[0] = jnp.concatenate([parts[s, 0] for s in range(parts.shape[0])], 1)


def merged(parts):
    segments, bins, channels, lanes = parts.shape
    return pl.pallas_call(
        merge_kernel,
        grid=(bins,),
        in_specs=[pl.BlockSpec((segments, 1, channels, lanes), lambda b: (0, b, 0, 0))],
        out_specs=pl.BlockSpec((1, channels, segments * lanes), lambda b: (b, 0, 0)),
        out_shape=jax.ShapeDtypeStruct((bins, channels, segments * lanes), parts.dtype),
        name="merge",
    )(parts)


def rotated(own):
    parts = []
    for s in range(own.shape[1] // LANES):
        tile = own[:, s * LANES : (s + 1) * LANES].astype(jnp.float32)
        lane = lax.broadcasted_iota(jnp.int32, tile.shape, 1)
        tile = pltpu.roll(tile, LANES // 2, 1)
        parts.append(jnp.where(lane < LANES // 2, tile, -tile).astype(jnp.bfloat16))
    return jnp.concatenate(parts, 1)


def cross_kernel(scale, own, others, out):
    mine = own[0]
    rows = mine.shape[0]
    left = jnp.concatenate([mine, rotated(mine)], 0)
    right = others[:, 0].reshape(others.shape[0] * rows, mine.shape[1])
    acc = lax.dot_general(left, right, (((1,), (1,)), ((), ())), preferred_element_type=jnp.float32)
    out[0] = (acc * scale).reshape(2, rows, acc.shape[1])


def cross(own, everyone, window_count):
    bins, rows, depth = own.shape
    devices = everyone.shape[0]
    return pl.pallas_call(
        functools.partial(cross_kernel, 1.0 / window_count),
        grid=(bins,),
        in_specs=[
            pl.BlockSpec((1, rows, depth), lambda b: (b, 0, 0)),
            pl.BlockSpec((devices, 1, rows, depth), lambda b: (0, b, 0, 0)),
        ],
        out_specs=pl.BlockSpec((1, 2, rows, devices * rows), lambda b: (b, 0, 0, 0)),
        out_shape=jax.ShapeDtypeStruct((bins, 2, rows, devices * rows), jnp.float32),
        compiler_params=pltpu.CompilerParams(vmem_limit_bytes=48 * 1024 * 1024),
        name="cross",
    )(own, everyone)


def local(strain_rate, window_starts):
    spectra = local_spectra(strain_rate, window_starts)
    segments = lax.axis_size("seg")
    channels = spectra.shape[1]
    parts = lax.all_to_all(spectra, "seg", split_axis=0, concat_axis=0, tiled=True)
    parts = parts.reshape(segments, F // segments, channels, LANES)
    own = merged(parts)
    everyone = lax.all_gather(own, "chan")
    return cross(own, everyone, segments * window_starts.shape[0])


def solution(mesh):
    in_specs = (P("chan", "seg"), P("seg"))
    out_specs = P("seg", None, "chan", None)
    return jax.shard_map(local, mesh=mesh, in_specs=in_specs, out_specs=out_specs, check_vma=False)
```

time: 430 us -> 315 us (0.73)
  local copies, waits for them, and re-layouts: 127 us -> 4.05 us
  Pallas kernels: 0 us -> 69 us
  other arithmetic: 29.2 us -> 0 us
  matrix products: 27.9 us -> 0 us
  blocking collectives: 46 us -> 37.7 us
  waiting for transfers between devices: 185 us -> 190 us
    reshape x3 -> x0, local copies, waits for them, and re-layouts: 70.3 us -> none  [the longest x1 60.2 us: cross_tile(): partner.reshape(partner.shape[0], partner.shape[1], partner.shape[2] * pa...]
    pallas_call x0 -> x3, Pallas kernels: none -> 69 us  [the longest x1 36.4 us: local_spectra(): pl.pallas_call(spectra_kernel, grid=(channels // GROUP,), in_specs=[pl.Bl...]
    all_gather x1 -> x0, local copies, waits for them, and re-layouts: 29.8 us -> none  [local(): lax.all_gather(operand, 'chan', axis=1, tiled=True)]
    dot_general x2 -> x0, matrix products: 27.9 us -> none  [the longest x1 23.3 us: cross_tile(): lax.dot_general(augmented, flat, (((2,), (2,)), ((0,), (0,))), preferred_...]
    unnamed x1 -> x0, other arithmetic: 16.6 us -> none
    gather x1 -> x0, local copies, waits for them, and re-layouts: 13.7 us -> none  [local_spectra(): jnp.take(blocks, block_index, axis=1)]
    all_to_all x1, blocking collectives: 46 us -> 37.7 us  [local(): lax.all_to_all(spectra, 'seg', split_axis=0, concat_axis=0, tiled=True)]
    reduce_sum x1 -> x0, other arithmetic: 8.23 us -> none  [local_spectra(): spread = jnp.sqrt(jnp.mean(windows * windows, -1, keepdims=True) + EPSILON)]
  transfers between devices with their start and end apart: 1 -> 1, of which waited for: 1 -> 1; matrix products, arithmetic and copies ran while one was open for 1% -> 0% of each run, Pallas kernels for 0% -> 0%
where the time goes in v1:
time: 315 us
  waiting for transfers between devices  190 us (60%)
  Pallas kernels  69 us (22%)
  blocking collectives  37.7 us (12%)
  between operations  13.4 us (4%)
  local copies, waits for them, and re-layouts  4.05 us (1%)
    all_gather x1, waiting for transfers between devices, local(): everyone = lax.all_gather(own, 'chan')  190 us
    all_to_all x1, blocking collectives, local(): lax.all_to_all(spectra, 'seg', split_axis=0, concat_axis=0, tiled=True)  37.7 us
    pallas_call x1, Pallas kernels, local_spectra(): pl.pallas_call(spectra_kernel, grid=(channels // GROUP,), in_specs=[pl.Bl...  36.4 us
    pallas_call x1, Pallas kernels, cross(): pl.pallas_call(functools.partial(cross_kernel, 1.0 / window_count), grid=...  25 us
    pallas_call x1, Pallas kernels, merged(): pl.pallas_call(merge_kernel, grid=(bins,), in_specs=[pl.BlockSpec((segmen...  7.64 us
  transfers between devices with their start and end apart: 1, of which 1 were waited for; matrix products, arithmetic and copies ran while one was open for 0% of the time, Pallas kernels for 0%

profile of v1, /device:TPU:1, one launch (start us, length us, event | category | flops | bytes accessed | tf_op | source)
XLA Modules:
  0.0 314.7 jit_solution(10851176862067938137)
XLA Ops:
  6.5 0.0 all-gather.3.cloned.1.call-start
  6.5 0.0 copy-start.1
  6.5 1.0 copy-done.1
  7.6 0.0 copy-start.2
  7.6 0.7 copy-done.2
  8.3 0.0 copy-start.3
  8.3 0.7 copy-done.3
  8.9 36.4 %spectra.1 = bf16[96,96,128]{2,1,0:T(8,128)(2,1)S(1)} custom-call(s32[64]{0:T(128)S(1)} %copy-done.3, bf16[96,33792]{1,0:T(8,128)(2,1)} %samples.1, bf16[1024,256]{1,0:T(8,128)(2,1)S(1)} %copy-done.1, f32[1,1024]{1,0:T(1,128)S(1)} %copy-done.2), custom_call_target="tpu_custom_call" | custom-call | tf_op jit(solution)/shard_map/spectra/pallas_call | solution.py:82
  45.3 37.7 %all_to_all.5 = bf16[96,96,128]{2,1,0:T(8,128)(2,1)} all-to-all(bf16[96,96,128]{2,1,0:T(8,128)(2,1)S(1)} %spectra.1), channel_id=1, replica_groups=mesh['chan'=16,'seg'=8] {'seg'}, dimensions={0} | all-to-all | bytes 4718592 | tf_op jit(solution)/shard_map/all_to_all | solution.py:160
  83.0 7.6 %merge.1.own = bf16[12,96,1024]{2,1,0:T(8,128)(2,1)} custom-call(bf16[8,12,96,128]{3,2,1,0:T(8,128)(2,1)} %bitcast.3), custom_call_target="tpu_custom_call" | custom-call | tf_op jit(solution)/shard_map/merge/pallas_call | solution.py:110
  90.7 0.0 all-gather.3.cloned.1.call-update
  90.7 190.5 %all-gather.3.cloned.1.call-done = bf16[192,96,1024]{2,1,0:T(8,128)(2,1)} async-done(((bf16[12,96,1024]{2,1,0:T(8,128)(2,1)}), bf16[192,96,1024]{2,1,0:T(8,128)(2,1)}) %all-gather.3.cloned.1.call-update) | async-done | bytes 37748752 | tf_op jit(solution)/shard_map/all_gather | solution.py:163
  281.2 0.0 copy-start
  281.2 1.7 copy-done
  282.8 25.0 %cross.1 = f32[12,2,96,1536]{3,2,1,0:T(8,128)} custom-call(bf16[12,96,1024]{2,1,0:T(8,128)(2,1)S(1)} %copy-done, bf16[16,12,96,1024]{3,2,1,0:T(8,128)(2,1)} %bitcast.2), custom_call_target="tpu_custom_call" | custom-call | tf_op jit(solution)/shard_map/cross/pallas_call | solution.py:142
Async XLA Ops:
  6.5 274.6 %all-gather.3.cloned.1.call-start = ((), (), s32[]{:S(2)}) async-start(), calls=%async_computation.1 | async-start | bytes 40108032 | tf_op jit(solution)/shard_map/all_gather | solution.py:163
  6.5 1.0 copy-start.1
  7.6 0.7 copy-start.2
  8.3 0.7 copy-start.3
  281.2 1.7 copy-start
Sparse Core Ops, SparseCore 0:
  90.8 190.3 all-gather.2

commit v2 on v1

v2 whole, which is shorter than its diff:
```python
import functools
import math

import jax
import jax.numpy as jnp
import numpy as np
from jax import lax
from jax.experimental import pallas as pl
from jax.experimental.pallas import tpu as pltpu
from jax.sharding import PartitionSpec as P
import ml_dtypes

WIN = 1024
QUARTER = WIN // 4
F = 96
K0 = 10
EPSILON = 1e-06
CLIP_LEVEL = 1.5
LANES = 128
GROUP = 32
BATCH = 16
STRIDE = 40


def fourier_columns():
    n = np.arange(WIN, dtype=np.int64)
    k = K0 + np.arange(F, dtype=np.int64)
    m = (n[:, None] * k[None, :]) % WIN
    phase = (m.astype(np.float32) * np.float32(2.0 * math.pi / WIN)).astype(np.float64)
    table = np.zeros((WIN, 2 * LANES), np.float32)
    table[:, :F] = np.cos(phase)
    table[:, LANES : LANES + F] = -np.sin(phase)
    return table.astype(ml_dtypes.bfloat16)


def hann_row():
    phase = (np.arange(WIN, dtype=np.float32) * np.float32(2.0 * math.pi / WIN)).astype(np.float64)
    return (0.5 - 0.5 * np.cos(phase)).astype(np.float32)[None, :]


def spectra_kernel(starts, samples, table, hann, out_b, out_a, taps, real, imag, staged):
    group = samples.shape[0]
    windows = starts.shape[0]

    def some_windows(i, _):
        for k in range(BATCH):
            first = pl.multiple_of(starts[i * BATCH + k] * QUARTER, QUARTER)
            win = samples[:, pl.ds(first, WIN)].astype(jnp.float32)
            power = jnp.sum(win * win, -1, keepdims=True) * (1.0 / WIN)
            level = CLIP_LEVEL * jnp.sqrt(power + EPSILON)
            tap = jnp.clip(win, -level, level) * hann[...]
            taps[k * group : (k + 1) * group, :] = tap.astype(jnp.bfloat16)
        spec = jnp.dot(taps[...], table[...], preferred_element_type=jnp.float32)
        for k in range(BATCH):
            at = pl.ds(pl.multiple_of((i * BATCH + k) * STRIDE, 8), group)
            real[at, :] = spec[k * group : (k + 1) * group, :LANES]
            imag[at, :] = spec[k * group : (k + 1) * group, LANES:]
        return 0

    lax.fori_loop(0, windows // BATCH, some_windows, 0)

    def one_channel(c, _):
        at = pl.ds(c, windows, stride=STRIDE)
        both = jnp.concatenate([real[at, :], imag[at, :]], 0)
        turned = both.T[:F]
        total = jnp.sum(turned * turned, 0, keepdims=True)
        total = total + pltpu.roll(total, windows, 1)
        scale = lax.rsqrt(total * (1.0 / (2 * F)) + EPSILON)
        staged[pl.ds(c, F, stride=STRIDE), :] = turned * scale
        return 0

    lax.fori_loop(0, group, one_channel, 0, unroll=16)

    segments, first = out_b.shape[:2]
    bins = F // segments
    for s in range(segments):
        for b in range(bins):
            value = staged[pl.ds((s * bins + b) * STRIDE, group), :].astype(jnp.bfloat16)
            if b < first:
                out_b[s, b] = value
            else:
                out_a[s, b - first] = value


def local_spectra(samples, starts, segments, first):
    channels, length = samples.shape
    windows = starts.shape[0]
    counts = (first, F // segments - first)
    return pl.pallas_call(
        spectra_kernel,
        grid=(channels // GROUP,),
        in_specs=[
            pl.BlockSpec(memory_space=pltpu.SMEM),
            pl.BlockSpec((GROUP, length), lambda g: (g, 0)),
            pl.BlockSpec((WIN, 2 * LANES), lambda g: (0, 0)),
            pl.BlockSpec((1, WIN), lambda g: (0, 0)),
        ],
        out_specs=[
            pl.BlockSpec((segments, n, GROUP, LANES), lambda g: (0, 0, g, 0)) for n in counts
        ],
        out_shape=[
            jax.ShapeDtypeStruct((segments, n, channels, LANES), jnp.bfloat16) for n in counts
        ],
        scratch_shapes=[
            pltpu.VMEM((BATCH * GROUP, WIN), jnp.bfloat16),
            pltpu.VMEM((windows * STRIDE, LANES), jnp.float32),
            pltpu.VMEM((windows * STRIDE, LANES), jnp.float32),
            pltpu.VMEM((F * STRIDE, LANES), jnp.float32),
        ],
        compiler_params=pltpu.CompilerParams(vmem_limit_bytes=48 * 1024 * 1024),
        name="spectra",
    )(starts, samples, jnp.asarray(fourier_columns()), jnp.asarray(hann_row()))


def rotated(own):
    parts = []
    for s in range(own.shape[1] // LANES):
        tile = own[:, s * LANES : (s + 1) * LANES].astype(jnp.float32)
        lane = lax.broadcasted_iota(jnp.int32, tile.shape, 1)
        tile = pltpu.roll(tile, LANES // 2, 1)
        parts.append(jnp.where(lane < LANES // 2, tile, -tile).astype(jnp.bfloat16))
    return jnp.concatenate(parts, 1)


def after_kernel(*refs):
    del refs


def together(*values):
    return pl.pallas_call(
        after_kernel,
        in_specs=[pl.BlockSpec(memory_space=pl.ANY)] * len(values),
        out_specs=[pl.BlockSpec(memory_space=pl.ANY)] * len(values),
        out_shape=[jax.ShapeDtypeStruct(v.shape, v.dtype) for v in values],
        input_output_aliases={i: i for i in range(len(values))},
        name="together",
    )(*values)


def after(value, *first):
    return pl.pallas_call(
        after_kernel,
        in_specs=[pl.BlockSpec(memory_space=pl.ANY)] * (1 + len(first)),
        out_specs=pl.BlockSpec(memory_space=pl.ANY),
        out_shape=jax.ShapeDtypeStruct(value.shape, value.dtype),
        input_output_aliases={0: 0},
        name="after",
    )(value, *first)


def stack(scale, own, right):
    segments, rows = own.shape[0], own.shape[2]
    mine = jnp.concatenate([own[s, 0] for s in range(segments)], 1)
    left = jnp.concatenate([mine, rotated(mine)], 0)
    acc = lax.dot_general(left, right, (((1,), (1,)), ((), ())), preferred_element_type=jnp.float32)
    return (acc * scale).reshape(2, rows, acc.shape[1])


def gathered_kernel(scale, place, own, others, *refs):
    del place
    segments = own.shape[0]
    columns = others.shape[0] * others.shape[3]
    right = [others[:, s, 0].reshape(columns, LANES) for s in range(segments)]
    refs[-1][0] = stack(scale, own, jnp.concatenate(right, 1))


def pieces_kernel(scale, place, own, *refs):
    pieces = refs[:8]
    out, buf, sems = refs[-3:]
    step = pl.program_id(0)
    z, core = place[1], place[2]

    def copies(b, slot):
        made = []
        for c in range(2):
            for i in range(4):
                at = lax.rem(z + i, 4) * 2 + (core if c == 0 else 1 - core)
                made.append(
                    pltpu.make_async_copy(
                        pieces[4 * c + i].at[:, b], buf.at[slot, at], sems.at[slot, 4 * c + i]
                    )
                )
        return made

    slot = lax.rem(step, 2)

    @pl.when(step == 0)
    def _():
        for copy in copies(0, 0):
            copy.start()

    @pl.when(step + 1 < pl.num_programs(0))
    def _():
        for copy in copies(step + 1, 1 - slot):
            copy.start()

    for copy in copies(step, slot):
        copy.wait()

    segments = own.shape[0]
    columns = buf.shape[1] * buf.shape[3]
    right = [buf[slot, :, s].reshape(columns, LANES) for s in range(segments)]
    out[0] = stack(scale, own, jnp.concatenate(right, 1))


def cross(place, own, others, base, first_bin, *, all_bins, chan, window_count):
    segments, bins, rows, lanes = own.shape
    half = chan // 2
    bases = [] if base is None else [base]
    anywhere = pl.BlockSpec(memory_space=pl.ANY)
    if isinstance(others, list):
        kernel = pieces_kernel
        specs = [anywhere] * len(others)
        scratch = [
            pltpu.VMEM((2, half, segments, rows, lanes), own.dtype),
            pltpu.SemaphoreType.DMA((2, len(others))),
        ]
    else:
        kernel = gathered_kernel
        specs = [pl.BlockSpec((half, segments, 1, rows, lanes), lambda b, at: (0, 0, b, 0, 0))]
        others = [others]
        scratch = []
    return pl.pallas_call(
        functools.partial(kernel, 1.0 / window_count),
        grid_spec=pltpu.PrefetchScalarGridSpec(
            num_scalar_prefetch=1,
            grid=(bins,),
            in_specs=[pl.BlockSpec((segments, 1, rows, lanes), lambda b, at: (0, b, 0, 0))]
            + specs
            + [anywhere] * len(bases),
            out_specs=pl.BlockSpec(
                (1, 2, rows, half * rows), lambda b, at: (b + first_bin, 0, 0, at[0])
            ),
            scratch_shapes=scratch,
        ),
        out_shape=jax.ShapeDtypeStruct((all_bins, 2, rows, chan * rows), jnp.float32),
        input_output_aliases={2 + len(others): 0} if bases else {},
        compiler_params=pltpu.CompilerParams(vmem_limit_bytes=56 * 1024 * 1024),
        cost_estimate=pl.CostEstimate(
            flops=4 * bins * rows * half * rows * segments * lanes,
            bytes_accessed=bins * half * rows * (2 * segments * lanes + 8 * rows),
            transcendentals=0,
        ),
        name="cross",
    )(place, own, *others, *bases)


def chan_index(x, z, c):
    return x * 8 + z * 2 + c


PLACES = [(x, z, c) for x in range(2) for z in range(4) for c in range(2)]
ACROSS = [(chan_index(x, z, c), chan_index(1 - x, z, c)) for x, z, c in PLACES]
SIBLING = [(chan_index(x, z, c), chan_index(x, z, 1 - c)) for x, z, c in PLACES]
X_HALVES = [list(range(8)), list(range(8, 16))]


def send(value, pairs):
    return lax.ppermute(value, "chan", pairs)


def gather(value):
    return lax.all_gather(value, "chan", axis_index_groups=X_HALVES)


def exchange(value):
    return lax.all_to_all(value, "seg", split_axis=0, concat_axis=0, tiled=True)


FIRST = 7


def local(strain_rate, window_starts):
    segments = lax.axis_size("seg")
    chan = lax.axis_size("chan")
    bins = F // segments
    spectra_b, spectra_a = local_spectra(strain_rate, window_starts, segments, FIRST)
    me = lax.axis_index("chan")
    z = lax.rem(me // 2, 4)
    core = lax.rem(me, 2)
    near = jnp.stack([me // 8, z, core])
    far = jnp.stack([1 - me // 8, z, core])

    count = segments * window_starts.shape[0]
    stacked = functools.partial(cross, all_bins=bins, chan=chan, window_count=count)

    own_b = exchange(spectra_b)
    all_b = gather(own_b)
    far_b = [send(own_b, ACROSS)]
    own_a = after(exchange(spectra_a), far_b[0])
    far_a = send(own_a, ACROSS)
    all_a = gather(own_a)
    all_far_a = gather(far_a)
    for hop in range(1, 4):
        at = lax.rem(z + hop, 4) * 2 + core
        far_b.append(send(lax.dynamic_index_in_dim(all_b, at, 0, keepdims=False), ACROSS))
    out = stacked(after(near, far_b[1]), own_b, all_b, None, 0)
    out = stacked(near, own_a, all_a, out, FIRST)
    out, last = together(out, far_b[3])
    far_b = far_b + [send(p, SIBLING) for p in (*far_b[:3], last)]
    out = stacked(far, own_b, far_b, out, 0)
    return stacked(far, own_a, all_far_a, out, FIRST)


def solution(mesh):
    in_specs = (P("chan", "seg"), P("seg"))
    out_specs = P("seg", None, "chan", None)
    return jax.shard_map(local, mesh=mesh, in_specs=in_specs, out_specs=out_specs, check_vma=False)
```

time: 315 us -> 244 us (0.77)
  waiting for transfers between devices: 190 us -> 73.5 us
  blocking collectives: 37.7 us -> 68.3 us
  starting transfers between devices: 0.01 us -> 18.5 us
  Pallas kernels: 69 us -> 56.5 us
  local copies, waits for them, and re-layouts: 4.05 us -> 12.1 us
    all_gather x1 -> x3, waiting for transfers between devices: 190 us -> 0.04 us  [gather(): return lax.all_gather(value, 'chan', axis_index_groups=X_HALVES)]
    ppermute x0 -> x9, waiting for transfers between devices: none -> 73.4 us  [send(): return lax.ppermute(value, 'chan', pairs)]
    all_to_all x1 -> x2, blocking collectives: 37.7 us -> 68.3 us  [exchange(): return lax.all_to_all(value, 'seg', split_axis=0, concat_axis=0, tiled=True)]
    pallas_call x1, Pallas kernels: 36.4 us -> 14.2 us  [local_spectra(): pl.pallas_call(spectra_kernel, grid=(channels // GROUP,), in_specs=[pl.Bl...]
    ppermute x0 -> x9, starting transfers between devices: none -> 18.4 us  [send(): return lax.ppermute(value, 'chan', pairs)]
    pallas_call x2 -> x7, Pallas kernels: 32.6 us -> 42.3 us  [the longest x4 42.3 us: cross(): pl.pallas_call(functools.partial(kernel, 1.0 / window_count), grid_spec=p...]
    squeeze x0 -> x1, local copies, waits for them, and re-layouts: none -> 4.25 us  [local(): lax.dynamic_index_in_dim(all_b, at, 0, keepdims=False)]
    unnamed x8 -> x22, local copies, waits for them, and re-layouts: 4.05 us -> 7.85 us
  transfers between devices with their start and end apart: 1 -> 12, of which waited for: 1 -> 5; matrix products, arithmetic and copies ran while one was open for 0% -> 3% of each run, Pallas kernels for 0% -> 14%
where the time goes in v2:
time: 244 us; the launch traced here: 243 us
  waiting for transfers between devices  73.5 us (30%)
  blocking collectives  68.3 us (28%)
  Pallas kernels  56.5 us (23%)
  starting transfers between devices  18.5 us (8%)
  between operations  13.2 us (5%)
  local copies, waits for them, and re-layouts  12.1 us (5%)
    ppermute x9, waiting for transfers between devices, send(): return lax.ppermute(value, 'chan', pairs)  73.4 us
    all_to_all x2, blocking collectives, exchange(): return lax.all_to_all(value, 'seg', split_axis=0, concat_axis=0, tiled=True)  68.3 us
    pallas_call x4, Pallas kernels, cross(): pl.pallas_call(functools.partial(kernel, 1.0 / window_count), grid_spec=p...  42.3 us
    ppermute x9, starting transfers between devices, send(): return lax.ppermute(value, 'chan', pairs)  18.4 us
    pallas_call x1, Pallas kernels, local_spectra(): pl.pallas_call(spectra_kernel, grid=(channels // GROUP,), in_specs=[pl.Bl...  14.2 us
    unnamed x22, local copies, waits for them, and re-layouts  7.85 us
  transfers between devices with their start and end apart: 12, of which 5 were waited for; matrix products, arithmetic and copies ran while one was open for 3% of the time, Pallas kernels for 14%

profile of v2, /device:TPU:1, one launch (start us, length us, event | category | flops | bytes accessed | tf_op | source)
XLA Modules:
  0.0 242.9 jit_solution(6957744820190975655)
XLA Ops:
  6.5 1.0 copy-done
  7.6 0.7 copy-done.1
  8.3 0.7 copy-done.2
  8.9 14.2 %spectra.1 = (bf16[8,7,96,128]{3,2,1,0:T(8,128)(2,1)S(1)}, bf16[8,5,96,128]{3,2,1,0:T(8,128)(2,1)S(1)}) custom-call(s32[64]{0:T(128)S(1)} %copy-done.2, bf16[96,33792]{1,0:T(8,128)(2,1)} %samples.1, bf16[1024,256]{1,0:T(8,128)(2,1)S(1)} %copy-done, f32[1,1024]{1,0:T(1,128)S(1)} %copy-done.1), custom_call_target="tpu_custom_call" | custom-call | tf_op jit(solution)/shard_map/spectra/pallas_call | solution.py:89
  23.2 26.9 %all_to_all.10.own = bf16[8,7,96,128]{3,2,1,0:T(8,128)(2,1)} all-to-all(bf16[8,7,96,128]{3,2,1,0:T(8,128)(2,1)S(1)} %get-tuple-element.10), channel_id=1, replica_groups=mesh['chan'=16,'seg'=8] {'seg'}, dimensions={0} | all-to-all | bytes 2752512 | tf_op jit(solution)/shard_map/all_to_all | solution.py:267
  50.1 1.3 copy-done.3
  51.4 0.4 collective-permute-start
  51.8 41.4 %all_to_all.11.refs_0_ = bf16[8,5,96,128]{3,2,1,0:T(8,128)(2,1)} all-to-all(bf16[8,5,96,128]{3,2,1,0:T(8,128)(2,1)S(1)} %get-tuple-element.9), channel_id=1, replica_groups=mesh['chan'=16,'seg'=8] {'seg'}, dimensions={0} | all-to-all | bytes 1966080 | tf_op jit(solution)/shard_map/all_to_all | solution.py:267
  93.3 0.1 collective-permute-start.1
  93.4 20.8 %collective-permute-done.1 = bf16[8,5,96,128]{3,2,1,0:T(8,128)(2,1)S(1)} collective-permute-done((bf16[8,5,96,128]{3,2,1,0:T(8,128)(2,1)}, bf16[8,5,96,128]{3,2,1,0:T(8,128)(2,1)S(1)}, u32[]{:S(2)}, u32[]{:S(2)}) %collective-permute-start.1) | collective-permute-done | bytes 983072 | tf_op jit(solution)/shard_map/ppermute | solution.py:259
  114.3 1.0 copy-done.8
  115.4 4.2 %dynamic-slice_bitcast_fusion = (bf16[8,7,96,128]{3,2,1,0:T(8,128)(2,1)}, bf16[8,7,96,128]{3,2,1,0:T(8,128)(2,1)}, bf16[8,7,96,128]{3,2,1,0:T(8,128)(2,1)}) fusion(bf16[8,8,7,96,128]{4,3,2,1,0:T(8,128)(2,1)} %bitcast.13, s32[]{:T(128)S(6)} %select_n.23, s32[]{:T(128)S(6)} %select_n.22, s32[]{:T(128)S(6)} %select_n.21), kind=kLoop, calls=%fused_computation | loop fusion | bytes 8257548 | tf_op jit(solution)/shard_map/jit(dynamic_index_in_dim)/squeeze | solution.py:296
  119.6 0.1 collective-permute-start.4
  119.7 1.4 collective-permute-start.2
  121.2 0.1 add_add_fusion.1.place
  121.2 0.6 copy.13.refs_0_
  121.8 4.3 %collective-permute-start.5 = (bf16[8,7,96,128]{3,2,1,0:T(8,128)(2,1)}, bf16[8,7,96,128]{3,2,1,0:T(8,128)(2,1)}, u32[]{:S(2)}, u32[]{:S(2)}) collective-permute-start(bf16[8,7,96,128]{3,2,1,0:T(8,128)(2,1)} %collective-permute-done.refs_1_.refs_0_), channel_id=1, source_target_pairs={{0,8},{8,0},{16,24},{24,16},{32,40},{40,32},{48,56},{56,48},{64,72... | collective-permute-start | bytes 4128776 | tf_op jit(solution)/shard_map/ppermute | solution.py:259
  126.1 22.0 %collective-permute-done.4.refs_3_ = bf16[8,7,96,128]{3,2,1,0:T(8,128)(2,1)S(1)} collective-permute-done((bf16[8,7,96,128]{3,2,1,0:T(8,128)(2,1)}, bf16[8,7,96,128]{3,2,1,0:T(8,128)(2,1)S(1)}, u32[]{:S(2)}, u32[]{:S(2)}) %collective-permute-start.4) | collective-permute-done | bytes 1376288 | tf_op jit(solution)/shard_map/ppermute | solution.py:259
  148.1 1.1 copy.16.refs_1_
  149.3 0.4 copy-done.4
  149.7 27.9 %collective-permute-done.2.refs_1_ = bf16[8,7,96,128]{3,2,1,0:T(8,128)(2,1)S(1)} collective-permute-done((bf16[8,7,96,128]{3,2,1,0:T(8,128)(2,1)}, bf16[8,7,96,128]{3,2,1,0:T(8,128)(2,1)S(1)}, u32[]{:S(2)}, u32[]{:S(2)}) %collective-permute-start.2) | collective-permute-done | bytes 1376288 | tf_op jit(solution)/shard_map/ppermute | solution.py:259
  177.6 1.1 copy-done.5
  178.7 11.8 %cross.4.refs_0_ = f32[12,2,96,1536]{3,2,1,0:T(8,128)} custom-call(s32[3]{0:T(128)} %after.3.place, bf16[8,7,96,128]{3,2,1,0:T(8,128)(2,1)} %all_to_all.10.own, bf16[8,8,7,96,128]{4,3,2,1,0:T(8,128)(2,1)} %bitcast.14), custom_call_target="tpu_custom_call" | custom-call | flops 2113929216 | bytes 15138816 | tf_op jit(solution)/shard_map/cross/pallas_call | solution.py:223
  190.5 9.0 %cross.5.refs_0_ = f32[12,2,96,1536]{3,2,1,0:T(8,128)} custom-call(s32[3]{0:T(128)} %copy-done.9, bf16[8,5,96,128]{3,2,1,0:T(8,128)(2,1)} %after.2.own, bf16[8,8,5,96,128]{4,3,2,1,0:T(8,128)(2,1)} %bitcast.16, f32[12,2,96,1536]{3,2,1,0:T(8,128)} %cross.4.refs_0_), custom_call_target="tpu_custom_call", output_to_operand_aliasing={{}: (3, {})} | custom-call | flops 1509949440 | bytes 10813440 | tf_op jit(solution)/shard_map/cross/pallas_call | solution.py:223
  199.5 8.0 %collective-permute-start.8 = (bf16[8,7,96,128]{3,2,1,0:T(8,128)(2,1)}, bf16[8,7,96,128]{3,2,1,0:T(8,128)(2,1)S(1)}, u32[]{:S(2)}, u32[]{:S(2)}) collective-permute-start(bf16[8,7,96,128]{3,2,1,0:T(8,128)(2,1)} %get-tuple-element.11), channel_id=1, source_target_pairs={{0,8},{8,0},{16,24},{24,16},{32,40},{40,32},{48,56},{56,48},{64,72... | collective-permute-start | bytes 4128776 | tf_op jit(solution)/shard_map/ppermute | solution.py:259
  207.5 1.3 collective-permute-start.6
  208.8 2.7 %collective-permute-start.7 = (bf16[8,7,96,128]{3,2,1,0:T(8,128)(2,1)}, bf16[8,7,96,128]{3,2,1,0:T(8,128)(2,1)}, u32[]{:S(2)}, u32[]{:S(2)}) collective-permute-start(bf16[8,7,96,128]{3,2,1,0:T(8,128)(2,1)} %collective-permute-done.3.refs_2_), channel_id=1, source_target_pairs={{0,8},{8,0},{16,24},{24,16},{32,40},{40,32},{48,56},{56,48},{64,72... | collective-permute-start | bytes 4128776 | tf_op jit(solution)/shard_map/ppermute | solution.py:259
  211.5 0.7 add_add_fusion.place
  212.2 0.5 collective-permute-done.6.refs_5_
  212.7 2.2 collective-permute-done.7.refs_6_
  214.8 12.5 %cross.6.refs_0_ = f32[12,2,96,1536]{3,2,1,0:T(8,128)} custom-call(s32[3]{0:T(128)} %add_add_fusion.place, bf16[8,7,96,128]{3,2,1,0:T(8,128)(2,1)} %all_to_all.10.own, bf16[8,7,96,128]{3,2,1,0:T(8,128)(2,1)} %collective-permute-done.refs_1_.refs_0_, bf16[8,7,96,128]{3,2,1,0:T(8,128)(2,1)} %copy-done.5, ...), custom_call_target="tpu_custom_call", output_to_operand_aliasing={{}: (10, {})} | custom-call | flops 2113929216 | bytes 15138816 | tf_op jit(solution)/shard_map/cross/pallas_call | solution.py:223
  227.4 8.9 %cross.7 = f32[12,2,96,1536]{3,2,1,0:T(8,128)} custom-call(s32[3]{0:T(128)} %add_add_fusion.place, bf16[8,5,96,128]{3,2,1,0:T(8,128)(2,1)} %after.2.own, bf16[8,8,5,96,128]{4,3,2,1,0:T(8,128)(2,1)} %bitcast.15, f32[12,2,96,1536]{3,2,1,0:T(8,128)} %cross.6.refs_0_), custom_call_target="tpu_custom_call", output_to_operand_aliasing={{}: (3, {})} | custom-call | flops 1509949440 | bytes 10813440 | tf_op jit(solution)/shard_map/cross/pallas_call | solution.py:223
  (30 shorter events, 0.3 us)
Async XLA Ops:
  6.5 108.8 %all-gather.9.cloned.1.call-start = ((), (), s32[]{:S(2)}) async-start(), calls=%async_computation.3 | async-start | bytes 12386304 | tf_op jit(solution)/shard_map/all_gather | solution.py:263
  6.5 1.0 copy-start
  7.6 0.7 copy-start.1
  8.3 0.7 copy-start.2
  50.1 1.3 copy-start.3
  50.1 140.4 %all-gather.11.cloned.1.call-start = ((), (), s32[]{:S(2)}) async-start(), calls=%async_computation.4 | async-start | bytes 8847360 | tf_op jit(solution)/shard_map/all_gather | solution.py:263
  51.4 41.9 %collective-permute-start = (bf16[8,7,96,128]{3,2,1,0:T(8,128)(2,1)S(1)}, bf16[8,7,96,128]{3,2,1,0:T(8,128)(2,1)}, u32[]{:S(2)}, u32[]{:S(2)}) collective-permute-start(bf16[8,7,96,128]{3,2,1,0:T(8,128)(2,1)S(1)} %copy-done.3), channel_id=1, source_target_pairs={{0,64},{8,72},{16,80},{24,88},{32,96},{40,104},{48,112},{56,120},{... | collective-permute-start | bytes 4128776 | tf_op jit(solution)/shard_map/ppermute | solution.py:259
  93.3 134.1 %all-gather.7.cloned.1.call-start = ((), (), s32[]{:S(2)}) async-start(), calls=%async_computation.2 | async-start | bytes 8847360 | tf_op jit(solution)/shard_map/all_gather | solution.py:263
  93.3 20.9 %collective-permute-start.1 = (bf16[8,5,96,128]{3,2,1,0:T(8,128)(2,1)}, bf16[8,5,96,128]{3,2,1,0:T(8,128)(2,1)S(1)}, u32[]{:S(2)}, u32[]{:S(2)}) collective-permute-start(bf16[8,5,96,128]{3,2,1,0:T(8,128)(2,1)} %after.2.own), channel_id=1, source_target_pairs={{0,64},{8,72},{16,80},{24,88},{32,96},{40,104},{48,112},{56,120},{... | collective-permute-start | bytes 2949128 | tf_op jit(solution)/shard_map/ppermute | solution.py:259
  114.3 1.0 copy-start.8
  119.6 28.5 %collective-permute-start.4 = (bf16[8,7,96,128]{3,2,1,0:T(8,128)(2,1)}, bf16[8,7,96,128]{3,2,1,0:T(8,128)(2,1)S(1)}, u32[]{:S(2)}, u32[]{:S(2)}) collective-permute-start(bf16[8,7,96,128]{3,2,1,0:T(8,128)(2,1)} %get-tuple-element.13), channel_id=1, source_target_pairs={{0,64},{8,72},{16,80},{24,88},{32,96},{40,104},{48,112},{56,120},{... | collective-permute-start | bytes 4128776 | tf_op jit(solution)/shard_map/ppermute | solution.py:259
  119.7 57.9 %collective-permute-start.2 = (bf16[8,7,96,128]{3,2,1,0:T(8,128)(2,1)}, bf16[8,7,96,128]{3,2,1,0:T(8,128)(2,1)S(1)}, u32[]{:S(2)}, u32[]{:S(2)}) collective-permute-start(bf16[8,7,96,128]{3,2,1,0:T(8,128)(2,1)} %get-tuple-element.15), channel_id=1, source_target_pairs={{0,64},{8,72},{16,80},{24,88},{32,96},{40,104},{48,112},{56,120},{... | collective-permute-start | bytes 4128776 | tf_op jit(solution)/shard_map/ppermute | solution.py:259
  121.1 87.7 %collective-permute-start.3 = (bf16[8,7,96,128]{3,2,1,0:T(8,128)(2,1)}, bf16[8,7,96,128]{3,2,1,0:T(8,128)(2,1)}, u32[]{:S(2)}, u32[]{:S(2)}) collective-permute-start(bf16[8,7,96,128]{3,2,1,0:T(8,128)(2,1)} %get-tuple-element.14), channel_id=1, source_target_pairs={{0,64},{8,72},{16,80},{24,88},{32,96},{40,104},{48,112},{56,120},{... | collective-permute-start | bytes 4128776 | tf_op jit(solution)/shard_map/ppermute | solution.py:259
  121.2 28.0 %copy-start.9 = (s32[3]{0:T(128)}, s32[3]{0:T(128)S(1)}, u32[]{:S(2)}) copy-start(s32[3]{0:T(128)S(1)} %add_add_fusion.1.place) | copy-start | bytes 40
  121.8 90.4 %collective-permute-start.5 = (bf16[8,7,96,128]{3,2,1,0:T(8,128)(2,1)}, bf16[8,7,96,128]{3,2,1,0:T(8,128)(2,1)}, u32[]{:S(2)}, u32[]{:S(2)}) collective-permute-start(bf16[8,7,96,128]{3,2,1,0:T(8,128)(2,1)} %collective-permute-done.refs_1_.refs_0_), channel_id=1, source_target_pairs={{0,8},{8,0},{16,24},{24,16},{32,40},{40,32},{48,56},{56,48},{64,72... | collective-permute-start | bytes 4128776 | tf_op jit(solution)/shard_map/ppermute | solution.py:259
  148.1 1.6 copy-start.4
  177.6 1.1 copy-start.5
  199.5 8.0 %copy-start.6 = (bf16[8,7,96,128]{3,2,1,0:T(8,128)(2,1)S(1)}, bf16[8,7,96,128]{3,2,1,0:T(8,128)(2,1)}, u32[]{:S(2)}) copy-start(bf16[8,7,96,128]{3,2,1,0:T(8,128)(2,1)} %copy-done.5) | copy-start | bytes 4128772
  199.5 12.7 %collective-permute-start.8 = (bf16[8,7,96,128]{3,2,1,0:T(8,128)(2,1)}, bf16[8,7,96,128]{3,2,1,0:T(8,128)(2,1)S(1)}, u32[]{:S(2)}, u32[]{:S(2)}) collective-permute-start(bf16[8,7,96,128]{3,2,1,0:T(8,128)(2,1)} %get-tuple-element.11), channel_id=1, source_target_pairs={{0,8},{8,0},{16,24},{24,16},{32,40},{40,32},{48,56},{56,48},{64,72... | collective-permute-start | bytes 4128776 | tf_op jit(solution)/shard_map/ppermute | solution.py:259
  207.5 5.2 %collective-permute-start.6 = (bf16[8,7,96,128]{3,2,1,0:T(8,128)(2,1)S(1)}, bf16[8,7,96,128]{3,2,1,0:T(8,128)(2,1)}, u32[]{:S(2)}, u32[]{:S(2)}) collective-permute-start(bf16[8,7,96,128]{3,2,1,0:T(8,128)(2,1)S(1)} %copy-done.6), channel_id=1, source_target_pairs={{0,8},{8,0},{16,24},{24,16},{32,40},{40,32},{48,56},{56,48},{64,72... | collective-permute-start | bytes 4128776 | tf_op jit(solution)/shard_map/ppermute | solution.py:259
  208.8 6.0 %collective-permute-start.7 = (bf16[8,7,96,128]{3,2,1,0:T(8,128)(2,1)}, bf16[8,7,96,128]{3,2,1,0:T(8,128)(2,1)}, u32[]{:S(2)}, u32[]{:S(2)}) collective-permute-start(bf16[8,7,96,128]{3,2,1,0:T(8,128)(2,1)} %collective-permute-done.3.refs_2_), channel_id=1, source_target_pairs={{0,8},{8,0},{16,24},{24,16},{32,40},{40,32},{48,56},{56,48},{64,72... | collective-permute-start | bytes 4128776 | tf_op jit(solution)/shard_map/ppermute | solution.py:259
  212.2 2.6 %copy-start.7 = (bf16[8,7,96,128]{3,2,1,0:T(8,128)(2,1)}, bf16[8,7,96,128]{3,2,1,0:T(8,128)(2,1)S(1)}, u32[]{:S(2)}) copy-start(bf16[8,7,96,128]{3,2,1,0:T(8,128)(2,1)S(1)} %collective-permute-done.8.refs_7_) | copy-start | bytes 4128772
Sparse Core Ops, SparseCore 0:
  50.2 61.1 all-gather.8
  113.1 47.8 all-gather.10
  162.7 48.4 all-gather.6

commit v3 on v2

--- a/solution.py
+++ b/solution.py
@@ -267,7 +267,7 @@
     return lax.all_to_all(value, "seg", split_axis=0, concat_axis=0, tiled=True)
 
 
-FIRST = 7
+FIRST = 6
 
 
 def local(strain_rate, window_starts):

time: 244 us -> 234 us (0.959)
  blocking collectives: 68.3 us -> 64.5 us
  starting transfers between devices: 18.5 us -> 15.4 us
    all_to_all x2, blocking collectives: 68.3 us -> 64.5 us  [exchange(): return lax.all_to_all(value, 'seg', split_axis=0, concat_axis=0, tiled=True)]
    ppermute x9, starting transfers between devices: 18.4 us -> 15.3 us  [send(): return lax.ppermute(value, 'chan', pairs)]
    unnamed x22 -> x28, local copies, waits for them, and re-layouts: 7.85 us -> 9.76 us
  transfers between devices with their start and end apart: 12 -> 12, of which waited for: 5 -> 6; matrix products, arithmetic and copies ran while one was open for 3% -> 3% of each run, Pallas kernels for 14% -> 13%
where the time goes in v3:
time: 234 us; the launch traced here: 233 us
  waiting for transfers between devices  71.7 us (31%)
  blocking collectives  64.5 us (28%)
  Pallas kernels  54.2 us (23%)
  starting transfers between devices  15.4 us (7%)
  local copies, waits for them, and re-layouts  13.7 us (6%)
  between operations  13.2 us (6%)
    ppermute x9, waiting for transfers between devices, send(): return lax.ppermute(value, 'chan', pairs)  71.6 us
    all_to_all x2, blocking collectives, exchange(): return lax.all_to_all(value, 'seg', split_axis=0, concat_axis=0, tiled=True)  64.5 us
    pallas_call x4, Pallas kernels, cross(): pl.pallas_call(functools.partial(kernel, 1.0 / window_count), grid_spec=p...  40 us
    ppermute x9, starting transfers between devices, send(): return lax.ppermute(value, 'chan', pairs)  15.3 us
    pallas_call x1, Pallas kernels, local_spectra(): pl.pallas_call(spectra_kernel, grid=(channels // GROUP,), in_specs=[pl.Bl...  14.2 us
    unnamed x28, local copies, waits for them, and re-layouts  9.76 us
  transfers between devices with their start and end apart: 12, of which 6 were waited for; matrix products, arithmetic and copies ran while one was open for 3% of the time, Pallas kernels for 13%

profile of v3, /device:TPU:1, one launch (start us, length us, event | category | flops | bytes accessed | tf_op | source)
XLA Modules:
  0.0 233.4 jit_solution(16439967804119049704)
XLA Ops:
  6.5 1.0 copy-done
  7.6 0.7 copy-done.1
  8.3 0.7 copy-done.2
  8.9 14.2 %spectra.1 = (bf16[8,6,96,128]{3,2,1,0:T(8,128)(2,1)S(1)}, bf16[8,6,96,128]{3,2,1,0:T(8,128)(2,1)S(1)}) custom-call(s32[64]{0:T(128)S(1)} %copy-done.2, bf16[96,33792]{1,0:T(8,128)(2,1)} %samples.1, bf16[1024,256]{1,0:T(8,128)(2,1)S(1)} %copy-done, f32[1,1024]{1,0:T(1,128)S(1)} %copy-done.1), custom_call_target="tpu_custom_call" | custom-call | tf_op jit(solution)/shard_map/spectra/pallas_call | solution.py:89
  23.2 25.1 %all_to_all.10.own = bf16[8,6,96,128]{3,2,1,0:T(8,128)(2,1)} all-to-all(bf16[8,6,96,128]{3,2,1,0:T(8,128)(2,1)S(1)} %get-tuple-element.10), channel_id=1, replica_groups=mesh['chan'=16,'seg'=8] {'seg'}, dimensions={0} | all-to-all | bytes 2359296 | tf_op jit(solution)/shard_map/all_to_all | solution.py:267
  48.3 1.2 copy-done.4
  49.5 0.3 collective-permute-start
  49.9 39.4 %all_to_all.11.refs_0_ = bf16[8,6,96,128]{3,2,1,0:T(8,128)(2,1)} all-to-all(bf16[8,6,96,128]{3,2,1,0:T(8,128)(2,1)S(1)} %get-tuple-element.9), channel_id=1, replica_groups=mesh['chan'=16,'seg'=8] {'seg'}, dimensions={0} | all-to-all | bytes 2359296 | tf_op jit(solution)/shard_map/all_to_all | solution.py:267
  89.3 1.0 copy-done.5
  90.4 1.2 copy-done.3
  91.6 25.0 %collective-permute-done.1 = bf16[8,6,96,128]{3,2,1,0:T(8,128)(2,1)S(1)} collective-permute-done((bf16[8,6,96,128]{3,2,1,0:T(8,128)(2,1)S(1)}, bf16[8,6,96,128]{3,2,1,0:T(8,128)(2,1)S(1)}, u32[]{:S(2)}, u32[]{:S(2)}) %collective-permute-start.1) | collective-permute-done | bytes 1179680 | tf_op jit(solution)/shard_map/ppermute | solution.py:259
  116.5 1.1 copy-done.11
  117.7 4.0 %dynamic-slice_bitcast_fusion = (bf16[8,6,96,128]{3,2,1,0:T(8,128)(2,1)}, bf16[8,6,96,128]{3,2,1,0:T(8,128)(2,1)}, bf16[8,6,96,128]{3,2,1,0:T(8,128)(2,1)}) fusion(bf16[8,8,6,96,128]{4,3,2,1,0:T(8,128)(2,1)} %bitcast.13, s32[]{:T(128)S(6)} %select_n.23, s32[]{:T(128)S(6)} %select_n.22, s32[]{:T(128)S(6)} %select_n.21), kind=kLoop, calls=%fused_computation | loop fusion | bytes 7077900 | tf_op jit(solution)/shard_map/jit(dynamic_index_in_dim)/squeeze | solution.py:296
  121.7 0.2 collective-permute-start.4
  121.9 1.3 collective-permute-start.2
  123.4 0.5 copy.13.refs_0_
  123.9 4.1 %collective-permute-start.5 = (bf16[8,6,96,128]{3,2,1,0:T(8,128)(2,1)S(1)}, bf16[8,6,96,128]{3,2,1,0:T(8,128)(2,1)}, u32[]{:S(2)}, u32[]{:S(2)}) collective-permute-start(bf16[8,6,96,128]{3,2,1,0:T(8,128)(2,1)S(1)} %copy-done.6), channel_id=1, source_target_pairs={{0,8},{8,0},{16,24},{24,16},{32,40},{40,32},{48,56},{56,48},{64,72... | collective-permute-start | bytes 3538952 | tf_op jit(solution)/shard_map/ppermute | solution.py:259
  127.9 18.1 %collective-permute-done.4.refs_3_ = bf16[8,6,96,128]{3,2,1,0:T(8,128)(2,1)S(1)} collective-permute-done((bf16[8,6,96,128]{3,2,1,0:T(8,128)(2,1)}, bf16[8,6,96,128]{3,2,1,0:T(8,128)(2,1)S(1)}, u32[]{:S(2)}, u32[]{:S(2)}) %collective-permute-start.4) | collective-permute-done | bytes 1179680 | tf_op jit(solution)/shard_map/ppermute | solution.py:259
  146.0 1.0 copy.16.refs_1_
  147.1 0.4 copy-done.7
  147.4 23.8 %collective-permute-done.2.refs_1_ = bf16[8,6,96,128]{3,2,1,0:T(8,128)(2,1)S(1)} collective-permute-done((bf16[8,6,96,128]{3,2,1,0:T(8,128)(2,1)}, bf16[8,6,96,128]{3,2,1,0:T(8,128)(2,1)S(1)}, u32[]{:S(2)}, u32[]{:S(2)}) %collective-permute-start.2) | collective-permute-done | bytes 1179680 | tf_op jit(solution)/shard_map/ppermute | solution.py:259
  171.2 1.0 copy-done.8
  172.2 9.8 %cross.4.refs_0_ = f32[12,2,96,1536]{3,2,1,0:T(8,128)} custom-call(s32[3]{0:T(128)} %after.3.place, bf16[8,6,96,128]{3,2,1,0:T(8,128)(2,1)} %all_to_all.10.own, bf16[8,8,6,96,128]{4,3,2,1,0:T(8,128)(2,1)} %bitcast.14), custom_call_target="tpu_custom_call" | custom-call | flops 1811939328 | bytes 12976128 | tf_op jit(solution)/shard_map/cross/pallas_call | solution.py:223
  182.0 9.8 %cross.5.refs_0_ = f32[12,2,96,1536]{3,2,1,0:T(8,128)} custom-call(s32[3]{0:T(128)} %copy-done.12, bf16[8,6,96,128]{3,2,1,0:T(8,128)(2,1)} %after.2.own, bf16[8,8,6,96,128]{4,3,2,1,0:T(8,128)(2,1)} %bitcast.16, f32[12,2,96,1536]{3,2,1,0:T(8,128)} %cross.4.refs_0_), custom_call_target="tpu_custom_call", output_to_operand_aliasing={{}: (3, {})} | custom-call | flops 1811939328 | bytes 12976128 | tf_op jit(solution)/shard_map/cross/pallas_call | solution.py:223
  191.8 8.0 %collective-permute-start.8 = (bf16[8,6,96,128]{3,2,1,0:T(8,128)(2,1)}, bf16[8,6,96,128]{3,2,1,0:T(8,128)(2,1)S(1)}, u32[]{:S(2)}, u32[]{:S(2)}) collective-permute-start(bf16[8,6,96,128]{3,2,1,0:T(8,128)(2,1)} %get-tuple-element.11), channel_id=1, source_target_pairs={{0,8},{8,0},{16,24},{24,16},{32,40},{40,32},{48,56},{56,48},{64,72... | collective-permute-start | bytes 3538952 | tf_op jit(solution)/shard_map/ppermute | solution.py:259
  199.8 1.3 collective-permute-start.6
  201.1 0.6 add_add_fusion.place
  201.7 0.8 collective-permute-done.8.refs_7_
  202.5 3.7 %collective-permute-done.6.refs_5_ = bf16[8,6,96,128]{3,2,1,0:T(8,128)(2,1)} collective-permute-done((bf16[8,6,96,128]{3,2,1,0:T(8,128)(2,1)S(1)}, bf16[8,6,96,128]{3,2,1,0:T(8,128)(2,1)}, u32[]{:S(2)}, u32[]{:S(2)}) %collective-permute-start.6) | collective-permute-done | bytes 1179680 | tf_op jit(solution)/shard_map/ppermute | solution.py:259
  206.2 0.2 collective-permute-done.7.refs_6_
  206.5 10.8 %cross.6.refs_0_ = f32[12,2,96,1536]{3,2,1,0:T(8,128)} custom-call(s32[3]{0:T(128)} %add_add_fusion.place, bf16[8,6,96,128]{3,2,1,0:T(8,128)(2,1)} %all_to_all.10.own, bf16[8,6,96,128]{3,2,1,0:T(8,128)(2,1)} %copy-done.5, bf16[8,6,96,128]{3,2,1,0:T(8,128)(2,1)} %copy-done.8, ...), custom_call_target="tpu_custom_call", output_to_operand_aliasing={{}: (10, {})} | custom-call | flops 1811939328 | bytes 12976128 | tf_op jit(solution)/shard_map/cross/pallas_call | solution.py:223
  217.3 9.6 %cross.7 = f32[12,2,96,1536]{3,2,1,0:T(8,128)} custom-call(s32[3]{0:T(128)} %add_add_fusion.place, bf16[8,6,96,128]{3,2,1,0:T(8,128)(2,1)} %after.2.own, bf16[8,8,6,96,128]{4,3,2,1,0:T(8,128)(2,1)} %bitcast.15, f32[12,2,96,1536]{3,2,1,0:T(8,128)} %cross.6.refs_0_), custom_call_target="tpu_custom_call", output_to_operand_aliasing={{}: (3, {})} | custom-call | flops 1811939328 | bytes 12976128 | tf_op jit(solution)/shard_map/cross/pallas_call | solution.py:223
  (36 shorter events, 0.5 us)
Async XLA Ops:
  6.5 111.2 %all-gather.9.cloned.1.call-start = ((), (), s32[]{:S(2)}) async-start(), calls=%async_computation.3 | async-start | bytes 10616832 | tf_op jit(solution)/shard_map/all_gather | solution.py:263
  6.5 1.0 copy-start
  7.6 0.7 copy-start.1
  8.3 0.7 copy-start.2
  48.2 1.3 copy-start.4
  48.3 133.8 %all-gather.11.cloned.1.call-start = ((), (), s32[]{:S(2)}) async-start(), calls=%async_computation.4 | async-start | bytes 10616832 | tf_op jit(solution)/shard_map/all_gather | solution.py:263
  49.5 39.8 %collective-permute-start = (bf16[8,6,96,128]{3,2,1,0:T(8,128)(2,1)S(1)}, bf16[8,6,96,128]{3,2,1,0:T(8,128)(2,1)S(1)}, u32[]{:S(2)}, u32[]{:S(2)}) collective-permute-start(bf16[8,6,96,128]{3,2,1,0:T(8,128)(2,1)S(1)} %copy-done.4), channel_id=1, source_target_pairs={{0,64},{8,72},{16,80},{24,88},{32,96},{40,104},{48,112},{56,120},{... | collective-permute-start | bytes 3538952 | tf_op jit(solution)/shard_map/ppermute | solution.py:259
  89.3 1.0 copy-start.5
  90.3 1.3 copy-start.3
  90.3 126.9 %all-gather.7.cloned.1.call-start = ((), (), s32[]{:S(2)}) async-start(), calls=%async_computation.2 | async-start | bytes 10616832 | tf_op jit(solution)/shard_map/all_gather | solution.py:263
  91.6 25.0 %collective-permute-start.1 = (bf16[8,6,96,128]{3,2,1,0:T(8,128)(2,1)S(1)}, bf16[8,6,96,128]{3,2,1,0:T(8,128)(2,1)S(1)}, u32[]{:S(2)}, u32[]{:S(2)}) collective-permute-start(bf16[8,6,96,128]{3,2,1,0:T(8,128)(2,1)S(1)} %copy-done.3), channel_id=1, source_target_pairs={{0,64},{8,72},{16,80},{24,88},{32,96},{40,104},{48,112},{56,120},{... | collective-permute-start | bytes 3538952 | tf_op jit(solution)/shard_map/ppermute | solution.py:259
  116.5 1.1 copy-start.11
  117.7 6.2 %copy-start.6 = (bf16[8,6,96,128]{3,2,1,0:T(8,128)(2,1)S(1)}, bf16[8,6,96,128]{3,2,1,0:T(8,128)(2,1)}, u32[]{:S(2)}) copy-start(bf16[8,6,96,128]{3,2,1,0:T(8,128)(2,1)} %copy-done.5) | copy-start | bytes 3538948
  121.7 24.4 %collective-permute-start.4 = (bf16[8,6,96,128]{3,2,1,0:T(8,128)(2,1)}, bf16[8,6,96,128]{3,2,1,0:T(8,128)(2,1)S(1)}, u32[]{:S(2)}, u32[]{:S(2)}) collective-permute-start(bf16[8,6,96,128]{3,2,1,0:T(8,128)(2,1)} %get-tuple-element.13), channel_id=1, source_target_pairs={{0,64},{8,72},{16,80},{24,88},{32,96},{40,104},{48,112},{56,120},{... | collective-permute-start | bytes 3538952 | tf_op jit(solution)/shard_map/ppermute | solution.py:259
  121.9 49.4 %collective-permute-start.2 = (bf16[8,6,96,128]{3,2,1,0:T(8,128)(2,1)}, bf16[8,6,96,128]{3,2,1,0:T(8,128)(2,1)S(1)}, u32[]{:S(2)}, u32[]{:S(2)}) collective-permute-start(bf16[8,6,96,128]{3,2,1,0:T(8,128)(2,1)} %get-tuple-element.15), channel_id=1, source_target_pairs={{0,64},{8,72},{16,80},{24,88},{32,96},{40,104},{48,112},{56,120},{... | collective-permute-start | bytes 3538952 | tf_op jit(solution)/shard_map/ppermute | solution.py:259
  123.1 78.0 %collective-permute-start.3 = (bf16[8,6,96,128]{3,2,1,0:T(8,128)(2,1)}, bf16[8,6,96,128]{3,2,1,0:T(8,128)(2,1)}, u32[]{:S(2)}, u32[]{:S(2)}) collective-permute-start(bf16[8,6,96,128]{3,2,1,0:T(8,128)(2,1)} %get-tuple-element.14), channel_id=1, source_target_pairs={{0,64},{8,72},{16,80},{24,88},{32,96},{40,104},{48,112},{56,120},{... | collective-permute-start | bytes 3538952 | tf_op jit(solution)/shard_map/ppermute | solution.py:259
  123.4 23.7 %copy-start.12 = (s32[3]{0:T(128)}, s32[3]{0:T(128)S(1)}, u32[]{:S(2)}) copy-start(s32[3]{0:T(128)S(1)} %add_add_fusion.1.place) | copy-start | bytes 40
  123.9 77.8 %collective-permute-start.5 = (bf16[8,6,96,128]{3,2,1,0:T(8,128)(2,1)S(1)}, bf16[8,6,96,128]{3,2,1,0:T(8,128)(2,1)}, u32[]{:S(2)}, u32[]{:S(2)}) collective-permute-start(bf16[8,6,96,128]{3,2,1,0:T(8,128)(2,1)S(1)} %copy-done.6), channel_id=1, source_target_pairs={{0,8},{8,0},{16,24},{24,16},{32,40},{40,32},{48,56},{56,48},{64,72... | collective-permute-start | bytes 3538952 | tf_op jit(solution)/shard_map/ppermute | solution.py:259
  146.0 1.4 copy-start.7
  171.2 1.0 copy-start.8
  191.8 8.0 %copy-start.9 = (bf16[8,6,96,128]{3,2,1,0:T(8,128)(2,1)S(1)}, bf16[8,6,96,128]{3,2,1,0:T(8,128)(2,1)}, u32[]{:S(2)}) copy-start(bf16[8,6,96,128]{3,2,1,0:T(8,128)(2,1)} %copy-done.8) | copy-start | bytes 3538948
  191.8 10.7 %collective-permute-start.8 = (bf16[8,6,96,128]{3,2,1,0:T(8,128)(2,1)}, bf16[8,6,96,128]{3,2,1,0:T(8,128)(2,1)S(1)}, u32[]{:S(2)}, u32[]{:S(2)}) collective-permute-start(bf16[8,6,96,128]{3,2,1,0:T(8,128)(2,1)} %get-tuple-element.11), channel_id=1, source_target_pairs={{0,8},{8,0},{16,24},{24,16},{32,40},{40,32},{48,56},{56,48},{64,72... | collective-permute-start | bytes 3538952 | tf_op jit(solution)/shard_map/ppermute | solution.py:259
  199.8 6.4 %collective-permute-start.6 = (bf16[8,6,96,128]{3,2,1,0:T(8,128)(2,1)S(1)}, bf16[8,6,96,128]{3,2,1,0:T(8,128)(2,1)}, u32[]{:S(2)}, u32[]{:S(2)}) collective-permute-start(bf16[8,6,96,128]{3,2,1,0:T(8,128)(2,1)S(1)} %copy-done.9), channel_id=1, source_target_pairs={{0,8},{8,0},{16,24},{24,16},{32,40},{40,32},{48,56},{56,48},{64,72... | collective-permute-start | bytes 3538952 | tf_op jit(solution)/shard_map/ppermute | solution.py:259
  201.1 5.3 %collective-permute-start.7 = (bf16[8,6,96,128]{3,2,1,0:T(8,128)(2,1)}, bf16[8,6,96,128]{3,2,1,0:T(8,128)(2,1)}, u32[]{:S(2)}, u32[]{:S(2)}) collective-permute-start(bf16[8,6,96,128]{3,2,1,0:T(8,128)(2,1)} %collective-permute-done.3.refs_2_), channel_id=1, source_target_pairs={{0,8},{8,0},{16,24},{24,16},{32,40},{40,32},{48,56},{56,48},{64,72... | collective-permute-start | bytes 3538952 | tf_op jit(solution)/shard_map/ppermute | solution.py:259
  202.5 3.9 %copy-start.10 = (bf16[8,6,96,128]{3,2,1,0:T(8,128)(2,1)}, bf16[8,6,96,128]{3,2,1,0:T(8,128)(2,1)S(1)}, u32[]{:S(2)}) copy-start(bf16[8,6,96,128]{3,2,1,0:T(8,128)(2,1)S(1)} %collective-permute-done.8.refs_7_) | copy-start | bytes 3538948
Sparse Core Ops, SparseCore 0:
  48.4 54.2 all-gather.8
  104.4 54.4 all-gather.10
  160.5 54.4 all-gather.6

commit v4 on v3

--- a/solution.py
+++ b/solution.py
@@ -126,26 +126,16 @@
     del refs
 
 
-def together(*values):
+def after(first, *values):
+    anywhere = pl.BlockSpec(memory_space=pl.ANY)
     return pl.pallas_call(
         after_kernel,
-        in_specs=[pl.BlockSpec(memory_space=pl.ANY)] * len(values),
-        out_specs=[pl.BlockSpec(memory_space=pl.ANY)] * len(values),
+        in_specs=[anywhere] * (len(values) + len(first)),
+        out_specs=[anywhere] * len(values),
         out_shape=[jax.ShapeDtypeStruct(v.shape, v.dtype) for v in values],
         input_output_aliases={i: i for i in range(len(values))},
-        name="together",
-    )(*values)
-
-
-def after(value, *first):
-    return pl.pallas_call(
-        after_kernel,
-        in_specs=[pl.BlockSpec(memory_space=pl.ANY)] * (1 + len(first)),
-        out_specs=pl.BlockSpec(memory_space=pl.ANY),
-        out_shape=jax.ShapeDtypeStruct(value.shape, value.dtype),
-        input_output_aliases={0: 0},
         name="after",
-    )(value, *first)
+    )(*values, *first)
 
 
 def stack(scale, own, right):
@@ -164,8 +154,9 @@
     refs[-1][0] = stack(scale, own, jnp.concatenate(right, 1))
 
 
-def pieces_kernel(scale, place, own, *refs):
-    pieces = refs[:8]
+def pieces_kernel(scale, hops, place, own, *refs):
+    count = len(hops)
+    pieces = refs[: 2 * count]
     out, buf, sems = refs[-3:]
     step = pl.program_id(0)
     z, core = place[1], place[2]
@@ -173,13 +164,11 @@
     def copies(b, slot):
         made = []
         for c in range(2):
-            for i in range(4):
-                at = lax.rem(z + i, 4) * 2 + (core if c == 0 else 1 - core)
-                made.append(
-                    pltpu.make_async_copy(
-                        pieces[4 * c + i].at[:, b], buf.at[slot, at], sems.at[slot, 4 * c + i]
-                    )
-                )
+            for i, (hop, start) in enumerate(hops):
+                piece = pieces[count * c + i].at[:, b]
+                at = lax.rem(z + hop, 4) * 2 + (core if c == 0 else 1 - core)
+                to = buf.at[slot, at, pl.ds(start, piece.shape[0])]
+                made.append(pltpu.make_async_copy(piece, to, sems.at[slot, count * c + i]))
         return made
 
     slot = lax.rem(step, 2)
@@ -203,25 +192,25 @@
     out[0] = stack(scale, own, jnp.concatenate(right, 1))
 
 
-def cross(place, own, others, base, first_bin, *, all_bins, chan, window_count):
+def cross(place, own, others, base, first_bin, hops=None, *, all_bins, chan, window_count):
     segments, bins, rows, lanes = own.shape
     half = chan // 2
     bases = [] if base is None else [base]
     anywhere = pl.BlockSpec(memory_space=pl.ANY)
     if isinstance(others, list):
-        kernel = pieces_kernel
+        kernel = functools.partial(pieces_kernel, 1.0 / window_count, hops)
         specs = [anywhere] * len(others)
         scratch = [
             pltpu.VMEM((2, half, segments, rows, lanes), own.dtype),
             pltpu.SemaphoreType.DMA((2, len(others))),
         ]
     else:
-        kernel = gathered_kernel
+        kernel = functools.partial(gathered_kernel, 1.0 / window_count)
         specs = [pl.BlockSpec((half, segments, 1, rows, lanes), lambda b, at: (0, 0, b, 0, 0))]
         others = [others]
         scratch = []
     return pl.pallas_call(
-        functools.partial(kernel, 1.0 / window_count),
+        kernel,
         grid_spec=pltpu.PrefetchScalarGridSpec(
             num_scalar_prefetch=1,
             grid=(bins,),
@@ -250,6 +239,8 @@
 
 
 PLACES = [(x, z, c) for x in range(2) for z in range(4) for c in range(2)]
+UP = [(chan_index(x, z, c), chan_index(x, (z + 1) % 4, c)) for x, z, c in PLACES]
+DOWN = [(chan_index(x, z, c), chan_index(x, (z + 3) % 4, c)) for x, z, c in PLACES]
 ACROSS = [(chan_index(x, z, c), chan_index(1 - x, z, c)) for x, z, c in PLACES]
 SIBLING = [(chan_index(x, z, c), chan_index(x, z, 1 - c)) for x, z, c in PLACES]
 X_HALVES = [list(range(8)), list(range(8, 16))]
@@ -268,6 +259,7 @@
 
 
 FIRST = 6
+SPLIT = 4
 
 
 def local(strain_rate, window_starts):
@@ -284,22 +276,36 @@
     count = segments * window_starts.shape[0]
     stacked = functools.partial(cross, all_bins=bins, chan=chan, window_count=count)
 
+    half = segments // 2
+    ring = [(0, 0), (3, 0), (1, 0), (2, 0), (2, half)]
+
     own_b = exchange(spectra_b)
     all_b = gather(own_b)
     far_b = [send(own_b, ACROSS)]
-    own_a = after(exchange(spectra_a), far_b[0])
-    far_a = send(own_a, ACROSS)
-    all_a = gather(own_a)
-    all_far_a = gather(far_a)
-    for hop in range(1, 4):
-        at = lax.rem(z + hop, 4) * 2 + core
-        far_b.append(send(lax.dynamic_index_in_dim(all_b, at, 0, keepdims=False), ACROSS))
-    out = stacked(after(near, far_b[1]), own_b, all_b, None, 0)
-    out = stacked(near, own_a, all_a, out, FIRST)
-    out, last = together(out, far_b[3])
-    far_b = far_b + [send(p, SIBLING) for p in (*far_b[:3], last)]
-    out = stacked(far, own_b, far_b, out, 0)
-    return stacked(far, own_a, all_far_a, out, FIRST)
+    (own_a,) = after([far_b[0]], exchange(spectra_a))
+    own_a1, own_a2 = own_a[:, :SPLIT], own_a[:, SPLIT:]
+    x_a = send(own_a, ACROSS)
+    all_a1 = gather(own_a1)
+    up_a2, down_a2 = send(own_a2, UP), send(own_a2, DOWN)
+    hops = [
+        lax.dynamic_index_in_dim(all_b, lax.rem(z + hop, 4) * 2 + core, 0, keepdims=False)
+        for hop in range(1, 4)
+    ]
+    x_a, *hops = after([], x_a, *hops)
+    all_xa = gather(x_a)
+    far_b = far_b + [send(hop, ACROSS) for hop in hops]
+    near_a2 = [own_a2, up_a2, down_a2, send(up_a2[:half], UP), send(down_a2[half:], DOWN)]
+    near_a2 = near_a2 + [send(p, SIBLING) for p in near_a2]
+
+    (near,) = after([far_b[1]], near)
+    out = stacked(near, own_b, all_b, None, 0)
+    out = stacked(near, own_a1, all_a1, out, FIRST)
+    out = stacked(near, own_a2, near_a2, out, FIRST + SPLIT, ring)
+    out, last = after([], out, far_b[3])
+    far_b[3] = last
+    far_b = far_b + [send(p, SIBLING) for p in far_b]
+    out = stacked(far, own_b, far_b, out, 0, [(0, 0), (1, 0), (2, 0), (3, 0)])
+    return stacked(far, own_a, all_xa, out, FIRST)
 
 
 def solution(mesh):

time: 234 us -> 230 us (0.983)
  waiting for transfers between devices: 71.7 us -> 53.4 us
  starting transfers between devices: 15.4 us -> 21.6 us
  local copies, waits for them, and re-layouts: 13.7 us -> 17.6 us
  Pallas kernels: 54.2 us -> 57.3 us
    ppermute x9 -> x18, waiting for transfers between devices: 71.6 us -> 43.1 us  [send(): return lax.ppermute(value, 'chan', pairs)]
    all_gather x3, waiting for transfers between devices: 0.04 us -> 10.3 us  [gather(): return lax.all_gather(value, 'chan', axis_index_groups=X_HALVES)]
    ppermute x9 -> x18, starting transfers between devices: 15.3 us -> 21.5 us  [send(): return lax.ppermute(value, 'chan', pairs)]
    slice x0 -> x4, local copies, waits for them, and re-layouts: none -> 3.85 us  [the longest x2 2.22 us: local(): own_a1, own_a2 = (own_a[:, :SPLIT], own_a[:, SPLIT:])]
    pallas_call x7 -> x9, Pallas kernels: 40 us -> 43.1 us  [the longest x5 43.1 us: cross(): pl.pallas_call(kernel, grid_spec=pltpu.PrefetchScalarGridSpec(num_scalar_...]
    unnamed x28 -> x36, local copies, waits for them, and re-layouts: 9.76 us -> 9.89 us
  transfers between devices with their start and end apart: 12 -> 21, of which waited for: 6 -> 9; matrix products, arithmetic and copies ran while one was open for 3% -> 4% of each run, Pallas kernels for 13% -> 15%
where the time goes in v4:
time: 230 us; the launch traced here: 229 us
  blocking collectives  64.5 us (28%)
  Pallas kernels  57.3 us (25%)
  waiting for transfers between devices  53.4 us (23%)
  starting transfers between devices  21.6 us (9%)
  local copies, waits for them, and re-layouts  17.6 us (8%)
  between operations  13.3 us (6%)
    all_to_all x2, blocking collectives, exchange(): return lax.all_to_all(value, 'seg', split_axis=0, concat_axis=0, tiled=True)  64.5 us
    pallas_call x5, Pallas kernels, cross(): pl.pallas_call(kernel, grid_spec=pltpu.PrefetchScalarGridSpec(num_scalar_...  43.1 us
    ppermute x18, waiting for transfers between devices, send(): return lax.ppermute(value, 'chan', pairs)  43.1 us
    ppermute x18, starting transfers between devices, send(): return lax.ppermute(value, 'chan', pairs)  21.5 us
    pallas_call x1, Pallas kernels, local_spectra(): pl.pallas_call(spectra_kernel, grid=(channels // GROUP,), in_specs=[pl.Bl...  14.2 us
    all_gather x3, waiting for transfers between devices, gather(): return lax.all_gather(value, 'chan', axis_index_groups=X_HALVES)  10.3 us
    unnamed x36, local copies, waits for them, and re-layouts  9.89 us
  transfers between devices with their start and end apart: 21, of which 9 were waited for; matrix products, arithmetic and copies ran while one was open for 4% of the time, Pallas kernels for 15%

profile of v4, /device:TPU:1, one launch (start us, length us, event | category | flops | bytes accessed | tf_op | source)
XLA Modules:
  0.0 228.9 jit_solution(15013673097449311448)
XLA Ops:
  6.5 1.0 copy-done
  8.9 14.2 %spectra.1 = (bf16[8,6,96,128]{3,2,1,0:T(8,128)(2,1)S(1)}, bf16[8,6,96,128]{3,2,1,0:T(8,128)(2,1)S(1)}) custom-call(s32[64]{0:T(128)S(1)} %copy-done.2, bf16[96,33792]{1,0:T(8,128)(2,1)} %samples.1, bf16[1024,256]{1,0:T(8,128)(2,1)S(1)} %copy-done, f32[1,1024]{1,0:T(1,128)S(1)} %copy-done.1), custom_call_target="tpu_custom_call" | custom-call | tf_op jit(solution)/shard_map/spectra/pallas_call | solution.py:89
  23.1 25.1 %all_to_all.10.own = bf16[8,6,96,128]{3,2,1,0:T(8,128)(2,1)} all-to-all(bf16[8,6,96,128]{3,2,1,0:T(8,128)(2,1)S(1)} %get-tuple-element.14), channel_id=1, replica_groups=mesh['chan'=16,'seg'=8] {'seg'}, dimensions={0} | all-to-all | bytes 2359296 | tf_op jit(solution)/shard_map/all_to_all | solution.py:258
  48.3 1.2 copy-done.4
  49.8 39.4 %all_to_all.11.refs_0_ = bf16[8,6,96,128]{3,2,1,0:T(8,128)(2,1)} all-to-all(bf16[8,6,96,128]{3,2,1,0:T(8,128)(2,1)S(1)} %get-tuple-element.13), channel_id=1, replica_groups=mesh['chan'=16,'seg'=8] {'seg'}, dimensions={0} | all-to-all | bytes 2359296 | tf_op jit(solution)/shard_map/all_to_all | solution.py:258
  90.3 2.2 slice.19.own
  92.7 10.0 %all-gather.7.cloned.1.call-done = bf16[64,6,96,128]{3,2,1,0:T(8,128)(2,1)} async-done(((bf16[8,6,96,128]{3,2,1,0:T(8,128)(2,1)}), bf16[64,6,96,128]{3,2,1,0:T(8,128)(2,1)}) %all-gather.7.cloned.1.call-update) | async-done | bytes 9437200 | tf_op jit(solution)/shard_map/all_gather | solution.py:254
  102.6 3.8 %dynamic-slice_bitcast_fusion = (bf16[8,6,96,128]{3,2,1,0:T(8,128)(2,1)}, bf16[8,6,96,128]{3,2,1,0:T(8,128)(2,1)}, bf16[8,6,96,128]{3,2,1,0:T(8,128)(2,1)}) fusion(bf16[8,8,6,96,128]{4,3,2,1,0:T(8,128)(2,1)} %bitcast.13, s32[]{:T(128)S(6)} %select_n.23, s32[]{:T(128)S(6)} %select_n.22, s32[]{:T(128)S(6)} %select_n.21), kind=kLoop, calls=%fused_computation | loop fusion | bytes 7077900 | tf_op jit(solution)/shard_map/jit(dynamic_index_in_dim)/squeeze | solution.py:291
  106.5 11.1 %collective-permute-done.1.refs_0_ = bf16[8,6,96,128]{3,2,1,0:T(8,128)(2,1)S(1)} collective-permute-done((bf16[8,6,96,128]{3,2,1,0:T(8,128)(2,1)S(1)}, bf16[8,6,96,128]{3,2,1,0:T(8,128)(2,1)S(1)}, u32[]{:S(2)}, u32[]{:S(2)}) %collective-permute-start.1) | collective-permute-done | bytes 1179680 | tf_op jit(solution)/shard_map/ppermute | solution.py:250
  117.6 1.0 copy-done.9
  118.7 1.2 copy-done.11
  120.0 1.9 collective-permute-start.4
  121.9 1.4 collective-permute-start.13
  123.3 2.2 collective-permute-start.5
  125.5 15.4 %collective-permute-done.4.refs_1_ = bf16[8,2,96,128]{3,2,1,0:T(8,128)(2,1)S(1)} collective-permute-done((bf16[8,2,96,128]{3,2,1,0:T(8,128)(2,1)S(1)}, bf16[8,2,96,128]{3,2,1,0:T(8,128)(2,1)S(1)}, u32[]{:S(2)}, u32[]{:S(2)}) %collective-permute-start.4) | collective-permute-done | bytes 393248 | tf_op jit(solution)/shard_map/ppermute | solution.py:250
  140.9 4.0 %collective-permute-start.8 = (bf16[8,2,96,128]{3,2,1,0:T(8,128)(2,1)S(1)}, bf16[8,2,96,128]{3,2,1,0:T(8,128)(2,1)S(1)}, u32[]{:S(2)}, u32[]{:S(2)}) collective-permute-start(bf16[8,2,96,128]{3,2,1,0:T(8,128)(2,1)S(1)} %slice.16.own.refs_0_), channel_id=1, source_target_pairs={{0,8},{8,0},{16,24},{24,16},{32,40},{40,32},{48,56},{56,48},{64,72... | collective-permute-start | bytes 1179656 | tf_op jit(solution)/shard_map/ppermute | solution.py:250
  145.0 1.2 collective-permute-done.8.refs_5_
  146.2 2.3 %collective-permute-start.10 = (bf16[8,2,96,128]{3,2,1,0:T(8,128)(2,1)}, bf16[8,2,96,128]{3,2,1,0:T(8,128)(2,1)}, u32[]{:S(2)}, u32[]{:S(2)}) collective-permute-start(bf16[8,2,96,128]{3,2,1,0:T(8,128)(2,1)} %collective-permute-done.5.refs_2_), channel_id=1, source_target_pairs={{0,8},{8,0},{16,24},{24,16},{32,40},{40,32},{48,56},{56,48},{64,72... | collective-permute-start | bytes 1179656 | tf_op jit(solution)/shard_map/ppermute | solution.py:250
  148.5 1.6 slice.18
  150.2 5.5 %collective-permute-done.6.refs_3_ = bf16[4,2,96,128]{3,2,1,0:T(8,128)(2,1)} collective-permute-done((bf16[4,2,96,128]{3,2,1,0:T(8,128)(2,1)S(1)}, bf16[4,2,96,128]{3,2,1,0:T(8,128)(2,1)}, u32[]{:S(2)}, u32[]{:S(2)}) %collective-permute-start.6) | collective-permute-done | bytes 196640 | tf_op jit(solution)/shard_map/ppermute | solution.py:250
  155.7 1.9 collective-permute-start.9
  158.2 3.0 %collective-permute-done.7.refs_4_ = bf16[4,2,96,128]{3,2,1,0:T(8,128)(2,1)} collective-permute-done((bf16[4,2,96,128]{3,2,1,0:T(8,128)(2,1)}, bf16[4,2,96,128]{3,2,1,0:T(8,128)(2,1)}, u32[]{:S(2)}, u32[]{:S(2)}) %collective-permute-start.7) | collective-permute-done | bytes 196640 | tf_op jit(solution)/shard_map/ppermute | solution.py:250
  161.2 2.1 collective-permute-start.11
  163.3 10.2 %cross.5.refs_0_ = f32[12,2,96,1536]{3,2,1,0:T(8,128)} custom-call(s32[3]{0:T(128)} %after.6.place, bf16[8,6,96,128]{3,2,1,0:T(8,128)(2,1)} %all_to_all.10.own, bf16[8,8,6,96,128]{4,3,2,1,0:T(8,128)(2,1)} %bitcast.14), custom_call_target="tpu_custom_call" | custom-call | flops 1811939328 | bytes 12976128 | tf_op jit(solution)/shard_map/cross/pallas_call | solution.py:212
  173.5 7.2 %cross.6.refs_10_ = f32[12,2,96,1536]{3,2,1,0:T(8,128)} custom-call(s32[3]{0:T(128)} %after.6.place, bf16[8,4,96,128]{3,2,1,0:T(8,128)(2,1)} %slice.19.own, bf16[8,8,4,96,128]{4,3,2,1,0:T(8,128)(2,1)} %bitcast.16, f32[12,2,96,1536]{3,2,1,0:T(8,128)} %cross.5.refs_0_), custom_call_target="tpu_custom_call", output_to_operand_aliasing={{}: (3, {})} | custom-call | flops 1207959552 | bytes 8650752 | tf_op jit(solution)/shard_map/cross/pallas_call | solution.py:212
  182.6 5.5 %cross.7.refs_0_ = f32[12,2,96,1536]{3,2,1,0:T(8,128)} custom-call(s32[3]{0:T(128)} %after.6.place, bf16[8,2,96,128]{3,2,1,0:T(8,128)(2,1)} %copy-done.12, bf16[8,2,96,128]{3,2,1,0:T(8,128)(2,1)} %copy-done.12, bf16[8,2,96,128]{3,2,1,0:T(8,128)(2,1)} %copy-done.14, ...), custom_call_target="tpu_custom_call", output_to_operand_aliasing={{}: (12, {})} | custom-call | flops 603979776 | bytes 4325376 | tf_op jit(solution)/shard_map/cross/pallas_call | solution.py:212
  188.1 1.0 copy-done.10
  189.9 4.7 %collective-permute-done.3.refs_2_ = bf16[8,6,96,128]{3,2,1,0:T(8,128)(2,1)} collective-permute-done((bf16[8,6,96,128]{3,2,1,0:T(8,128)(2,1)}, bf16[8,6,96,128]{3,2,1,0:T(8,128)(2,1)}, u32[]{:S(2)}, u32[]{:S(2)}) %collective-permute-start.3) | collective-permute-done | bytes 1179680 | tf_op jit(solution)/shard_map/ppermute | solution.py:250
  194.6 4.3 %collective-permute-start.16 = (bf16[8,6,96,128]{3,2,1,0:T(8,128)(2,1)}, bf16[8,6,96,128]{3,2,1,0:T(8,128)(2,1)}, u32[]{:S(2)}, u32[]{:S(2)}) collective-permute-start(bf16[8,6,96,128]{3,2,1,0:T(8,128)(2,1)} %collective-permute-done.3.refs_2_), channel_id=1, source_target_pairs={{0,8},{8,0},{16,24},{24,16},{32,40},{40,32},{48,56},{56,48},{64,72... | collective-permute-start | bytes 3538952 | tf_op jit(solution)/shard_map/ppermute | solution.py:250
  199.6 2.2 collective-permute-done.16.refs_6_
  201.8 10.7 %cross.8.refs_0_ = f32[12,2,96,1536]{3,2,1,0:T(8,128)} custom-call(s32[3]{0:T(128)} %add_add_fusion.place, bf16[8,6,96,128]{3,2,1,0:T(8,128)(2,1)} %all_to_all.10.own, bf16[8,6,96,128]{3,2,1,0:T(8,128)(2,1)} %copy-done.5, bf16[8,6,96,128]{3,2,1,0:T(8,128)(2,1)} %copy-done.7, ...), custom_call_target="tpu_custom_call", output_to_operand_aliasing={{}: (10, {})} | custom-call | flops 1811939328 | bytes 12976128 | tf_op jit(solution)/shard_map/cross/pallas_call | solution.py:212
  212.8 9.6 %cross.9 = f32[12,2,96,1536]{3,2,1,0:T(8,128)} custom-call(s32[3]{0:T(128)} %add_add_fusion.place, bf16[8,6,96,128]{3,2,1,0:T(8,128)(2,1)} %after.4.own, bf16[8,8,6,96,128]{4,3,2,1,0:T(8,128)(2,1)} %bitcast.15, f32[12,2,96,1536]{3,2,1,0:T(8,128)} %cross.8.refs_0_), custom_call_target="tpu_custom_call", output_to_operand_aliasing={{}: (3, {})} | custom-call | flops 1811939328 | bytes 12976128 | tf_op jit(solution)/shard_map/cross/pallas_call | solution.py:212
  (68 shorter events, 7.6 us)
Async XLA Ops:
  6.5 96.1 %all-gather.7.cloned.1.call-start = ((), (), s32[]{:S(2)}) async-start(), calls=%async_computation.2 | async-start | bytes 10616832 | tf_op jit(solution)/shard_map/all_gather | solution.py:254
  48.2 1.3 copy-start.4
  48.2 125.3 %all-gather.11.cloned.1.call-start = ((), (), s32[]{:S(2)}) async-start(), calls=%async_computation.4 | async-start | bytes 7077888 | tf_op jit(solution)/shard_map/all_gather | solution.py:254
  49.5 39.8 %collective-permute-start = (bf16[8,6,96,128]{3,2,1,0:T(8,128)(2,1)S(1)}, bf16[8,6,96,128]{3,2,1,0:T(8,128)(2,1)S(1)}, u32[]{:S(2)}, u32[]{:S(2)}) collective-permute-start(bf16[8,6,96,128]{3,2,1,0:T(8,128)(2,1)S(1)} %copy-done.4), channel_id=1, source_target_pairs={{0,64},{8,72},{16,80},{24,88},{32,96},{40,104},{48,112},{56,120},{... | collective-permute-start | bytes 3538952 | tf_op jit(solution)/shard_map/ppermute | solution.py:250
  90.3 2.3 copy-start.3
  92.5 120.3 %all-gather.9.cloned.1.call-start = ((), (), s32[]{:S(2)}) async-start(), calls=%async_computation.3 | async-start | bytes 10616832 | tf_op jit(solution)/shard_map/all_gather | solution.py:254
  92.5 25.1 %collective-permute-start.1 = (bf16[8,6,96,128]{3,2,1,0:T(8,128)(2,1)S(1)}, bf16[8,6,96,128]{3,2,1,0:T(8,128)(2,1)S(1)}, u32[]{:S(2)}, u32[]{:S(2)}) collective-permute-start(bf16[8,6,96,128]{3,2,1,0:T(8,128)(2,1)S(1)} %copy-done.3), channel_id=1, source_target_pairs={{0,64},{8,72},{16,80},{24,88},{32,96},{40,104},{48,112},{56,120},{... | collective-permute-start | bytes 3538952 | tf_op jit(solution)/shard_map/ppermute | solution.py:250
  118.6 1.3 copy-start.11
  119.9 35.8 %collective-permute-start.2 = (bf16[8,6,96,128]{3,2,1,0:T(8,128)(2,1)S(1)}, bf16[8,6,96,128]{3,2,1,0:T(8,128)(2,1)S(1)}, u32[]{:S(2)}, u32[]{:S(2)}) collective-permute-start(bf16[8,6,96,128]{3,2,1,0:T(8,128)(2,1)S(1)} %copy-done.11), channel_id=1, source_target_pairs={{0,64},{8,72},{16,80},{24,88},{32,96},{40,104},{48,112},{56,120},{... | collective-permute-start | bytes 3538952 | tf_op jit(solution)/shard_map/ppermute | solution.py:250
  120.0 20.9 %copy-start.12 = (bf16[8,2,96,128]{3,2,1,0:T(8,128)(2,1)}, bf16[8,2,96,128]{3,2,1,0:T(8,128)(2,1)S(1)}, u32[]{:S(2)}) copy-start(bf16[8,2,96,128]{3,2,1,0:T(8,128)(2,1)S(1)} %slice.16.own.refs_0_) | copy-start | bytes 1179652
  120.0 20.9 %collective-permute-start.4 = (bf16[8,2,96,128]{3,2,1,0:T(8,128)(2,1)S(1)}, bf16[8,2,96,128]{3,2,1,0:T(8,128)(2,1)S(1)}, u32[]{:S(2)}, u32[]{:S(2)}) collective-permute-start(bf16[8,2,96,128]{3,2,1,0:T(8,128)(2,1)S(1)} %slice.16.own.refs_0_), channel_id=1, source_target_pairs={{0,16},{8,24},{16,32},{24,40},{32,48},{40,56},{48,0},{56,8},{64,80... | collective-permute-start | bytes 1179656 | tf_op jit(solution)/shard_map/ppermute | solution.py:250
  121.9 66.2 %collective-permute-start.13 = (bf16[8,6,96,128]{3,2,1,0:T(8,128)(2,1)}, bf16[8,6,96,128]{3,2,1,0:T(8,128)(2,1)S(1)}, u32[]{:S(2)}, u32[]{:S(2)}) collective-permute-start(bf16[8,6,96,128]{3,2,1,0:T(8,128)(2,1)} %get-tuple-element.18), channel_id=1, source_target_pairs={{0,64},{8,72},{16,80},{24,88},{32,96},{40,104},{48,112},{56,120},{... | collective-permute-start | bytes 3538952 | tf_op jit(solution)/shard_map/ppermute | solution.py:250
  123.2 71.4 %collective-permute-start.3 = (bf16[8,6,96,128]{3,2,1,0:T(8,128)(2,1)}, bf16[8,6,96,128]{3,2,1,0:T(8,128)(2,1)}, u32[]{:S(2)}, u32[]{:S(2)}) collective-permute-start(bf16[8,6,96,128]{3,2,1,0:T(8,128)(2,1)} %get-tuple-element.17), channel_id=1, source_target_pairs={{0,64},{8,72},{16,80},{24,88},{32,96},{40,104},{48,112},{56,120},{... | collective-permute-start | bytes 3538952 | tf_op jit(solution)/shard_map/ppermute | solution.py:250
  123.3 21.6 %collective-permute-start.5 = (bf16[8,2,96,128]{3,2,1,0:T(8,128)(2,1)S(1)}, bf16[8,2,96,128]{3,2,1,0:T(8,128)(2,1)}, u32[]{:S(2)}, u32[]{:S(2)}) collective-permute-start(bf16[8,2,96,128]{3,2,1,0:T(8,128)(2,1)S(1)} %slice.16.own.refs_0_), channel_id=1, source_target_pairs={{0,48},{8,56},{16,0},{24,8},{32,16},{40,24},{48,32},{56,40},{64,11... | collective-permute-start | bytes 1179656 | tf_op jit(solution)/shard_map/ppermute | solution.py:250
  140.9 5.3 %copy-start.14 = (bf16[8,2,96,128]{3,2,1,0:T(8,128)(2,1)}, bf16[8,2,96,128]{3,2,1,0:T(8,128)(2,1)S(1)}, u32[]{:S(2)}) copy-start(bf16[8,2,96,128]{3,2,1,0:T(8,128)(2,1)S(1)} %collective-permute-done.4.refs_1_) | copy-start | bytes 1179652
  140.9 5.3 %collective-permute-start.8 = (bf16[8,2,96,128]{3,2,1,0:T(8,128)(2,1)S(1)}, bf16[8,2,96,128]{3,2,1,0:T(8,128)(2,1)S(1)}, u32[]{:S(2)}, u32[]{:S(2)}) collective-permute-start(bf16[8,2,96,128]{3,2,1,0:T(8,128)(2,1)S(1)} %slice.16.own.refs_0_), channel_id=1, source_target_pairs={{0,8},{8,0},{16,24},{24,16},{32,40},{40,32},{48,56},{56,48},{64,72... | collective-permute-start | bytes 1179656 | tf_op jit(solution)/shard_map/ppermute | solution.py:250
  144.9 10.7 %collective-permute-start.6 = (bf16[4,2,96,128]{3,2,1,0:T(8,128)(2,1)S(1)}, bf16[4,2,96,128]{3,2,1,0:T(8,128)(2,1)}, u32[]{:S(2)}, u32[]{:S(2)}) collective-permute-start(bf16[4,2,96,128]{3,2,1,0:T(8,128)(2,1)S(1)} %slice.17), channel_id=1, source_target_pairs={{0,16},{8,24},{16,32},{24,40},{32,48},{40,56},{48,0},{56,8},{64,80... | collective-permute-start | bytes 589832 | tf_op jit(solution)/shard_map/ppermute | solution.py:250
  146.2 2.3 %copy-start.15 = (bf16[8,2,96,128]{3,2,1,0:T(8,128)(2,1)}, bf16[8,2,96,128]{3,2,1,0:T(8,128)(2,1)S(1)}, u32[]{:S(2)}) copy-start(bf16[8,2,96,128]{3,2,1,0:T(8,128)(2,1)S(1)} %collective-permute-done.8.refs_5_) | copy-start | bytes 1179652
  146.2 17.1 %collective-permute-start.10 = (bf16[8,2,96,128]{3,2,1,0:T(8,128)(2,1)}, bf16[8,2,96,128]{3,2,1,0:T(8,128)(2,1)}, u32[]{:S(2)}, u32[]{:S(2)}) collective-permute-start(bf16[8,2,96,128]{3,2,1,0:T(8,128)(2,1)} %collective-permute-done.5.refs_2_), channel_id=1, source_target_pairs={{0,8},{8,0},{16,24},{24,16},{32,40},{40,32},{48,56},{56,48},{64,72... | collective-permute-start | bytes 1179656 | tf_op jit(solution)/shard_map/ppermute | solution.py:250
  155.7 5.5 %collective-permute-start.7 = (bf16[4,2,96,128]{3,2,1,0:T(8,128)(2,1)}, bf16[4,2,96,128]{3,2,1,0:T(8,128)(2,1)}, u32[]{:S(2)}, u32[]{:S(2)}) collective-permute-start(bf16[4,2,96,128]{3,2,1,0:T(8,128)(2,1)} %slice.18), channel_id=1, source_target_pairs={{0,48},{8,56},{16,0},{24,8},{32,16},{40,24},{48,32},{56,40},{64,11... | collective-permute-start | bytes 589832 | tf_op jit(solution)/shard_map/ppermute | solution.py:250
  155.7 2.5 %copy-start.7 = (bf16[8,6,96,128]{3,2,1,0:T(8,128)(2,1)}, bf16[8,6,96,128]{3,2,1,0:T(8,128)(2,1)S(1)}, u32[]{:S(2)}) copy-start(bf16[8,6,96,128]{3,2,1,0:T(8,128)(2,1)S(1)} %collective-permute-done.2.refs_1_) | copy-start | bytes 3538948
  155.7 25.0 %collective-permute-start.9 = (bf16[8,2,96,128]{3,2,1,0:T(8,128)(2,1)}, bf16[8,2,96,128]{3,2,1,0:T(8,128)(2,1)}, u32[]{:S(2)}, u32[]{:S(2)}) collective-permute-start(bf16[8,2,96,128]{3,2,1,0:T(8,128)(2,1)} %copy-done.14), channel_id=1, source_target_pairs={{0,8},{8,0},{16,24},{24,16},{32,40},{40,32},{48,56},{56,48},{64,72... | collective-permute-start | bytes 1179656 | tf_op jit(solution)/shard_map/ppermute | solution.py:250
  161.2 20.1 %collective-permute-start.11 = (bf16[4,2,96,128]{3,2,1,0:T(8,128)(2,1)}, bf16[4,2,96,128]{3,2,1,0:T(8,128)(2,1)S(1)}, u32[]{:S(2)}, u32[]{:S(2)}) collective-permute-start(bf16[4,2,96,128]{3,2,1,0:T(8,128)(2,1)} %collective-permute-done.6.refs_3_), channel_id=1, source_target_pairs={{0,8},{8,0},{16,24},{24,16},{32,40},{40,32},{48,56},{56,48},{64,72... | collective-permute-start | bytes 589832 | tf_op jit(solution)/shard_map/ppermute | solution.py:250
  163.3 18.0 %collective-permute-start.12 = (bf16[4,2,96,128]{3,2,1,0:T(8,128)(2,1)}, bf16[4,2,96,128]{3,2,1,0:T(8,128)(2,1)S(1)}, u32[]{:S(2)}, u32[]{:S(2)}) collective-permute-start(bf16[4,2,96,128]{3,2,1,0:T(8,128)(2,1)} %collective-permute-done.7.refs_4_), channel_id=1, source_target_pairs={{0,8},{8,0},{16,24},{24,16},{32,40},{40,32},{48,56},{56,48},{64,72... | collective-permute-start | bytes 589832 | tf_op jit(solution)/shard_map/ppermute | solution.py:250
  173.5 7.2 %copy-start.6 = (bf16[8,6,96,128]{3,2,1,0:T(8,128)(2,1)S(1)}, bf16[8,6,96,128]{3,2,1,0:T(8,128)(2,1)}, u32[]{:S(2)}) copy-start(bf16[8,6,96,128]{3,2,1,0:T(8,128)(2,1)} %copy-done.5) | copy-start | bytes 3538948
  180.7 18.9 %collective-permute-start.14 = (bf16[8,6,96,128]{3,2,1,0:T(8,128)(2,1)S(1)}, bf16[8,6,96,128]{3,2,1,0:T(8,128)(2,1)}, u32[]{:S(2)}, u32[]{:S(2)}) collective-permute-start(bf16[8,6,96,128]{3,2,1,0:T(8,128)(2,1)S(1)} %copy-done.6), channel_id=1, source_target_pairs={{0,8},{8,0},{16,24},{24,16},{32,40},{40,32},{48,56},{56,48},{64,72... | collective-permute-start | bytes 3538952 | tf_op jit(solution)/shard_map/ppermute | solution.py:250
  188.1 1.8 copy-start.8
  188.1 1.0 copy-start.10
  189.2 10.4 %collective-permute-start.17 = (bf16[8,6,96,128]{3,2,1,0:T(8,128)(2,1)}, bf16[8,6,96,128]{3,2,1,0:T(8,128)(2,1)S(1)}, u32[]{:S(2)}, u32[]{:S(2)}) collective-permute-start(bf16[8,6,96,128]{3,2,1,0:T(8,128)(2,1)} %get-tuple-element.19.refs_3_), channel_id=1, source_target_pairs={{0,8},{8,0},{16,24},{24,16},{32,40},{40,32},{48,56},{56,48},{64,72... | collective-permute-start | bytes 3538952 | tf_op jit(solution)/shard_map/ppermute | solution.py:250
  189.9 9.6 %collective-permute-start.15 = (bf16[8,6,96,128]{3,2,1,0:T(8,128)(2,1)S(1)}, bf16[8,6,96,128]{3,2,1,0:T(8,128)(2,1)}, u32[]{:S(2)}, u32[]{:S(2)}) collective-permute-start(bf16[8,6,96,128]{3,2,1,0:T(8,128)(2,1)S(1)} %copy-done.8), channel_id=1, source_target_pairs={{0,8},{8,0},{16,24},{24,16},{32,40},{40,32},{48,56},{56,48},{64,72... | collective-permute-start | bytes 3538952 | tf_op jit(solution)/shard_map/ppermute | solution.py:250
  194.6 7.2 %collective-permute-start.16 = (bf16[8,6,96,128]{3,2,1,0:T(8,128)(2,1)}, bf16[8,6,96,128]{3,2,1,0:T(8,128)(2,1)}, u32[]{:S(2)}, u32[]{:S(2)}) collective-permute-start(bf16[8,6,96,128]{3,2,1,0:T(8,128)(2,1)} %collective-permute-done.3.refs_2_), channel_id=1, source_target_pairs={{0,8},{8,0},{16,24},{24,16},{32,40},{40,32},{48,56},{56,48},{64,72... | collective-permute-start | bytes 3538952 | tf_op jit(solution)/shard_map/ppermute | solution.py:250
  199.6 2.2 copy-start.13
  (7 other events, 5.8 us)
Sparse Core Ops, SparseCore 0:
  48.4 54.2 all-gather.6
  104.3 52.2 all-gather.10
  158.3 54.3 all-gather.8

commit v5 on v4

--- a/solution.py
+++ b/solution.py
@@ -146,46 +146,50 @@
     return (acc * scale).reshape(2, rows, acc.shape[1])
 
 
-def gathered_kernel(scale, place, own, others, *refs):
-    del place
-    segments = own.shape[0]
-    columns = others.shape[0] * others.shape[3]
-    right = [others[:, s, 0].reshape(columns, LANES) for s in range(segments)]
-    refs[-1][0] = stack(scale, own, jnp.concatenate(right, 1))
-
-
-def pieces_kernel(scale, hops, place, own, *refs):
-    count = len(hops)
-    pieces = refs[: 2 * count]
+def cross_kernel(scale, hops, place, own, *refs):
     out, buf, sems = refs[-3:]
     step = pl.program_id(0)
+    steps = pl.num_programs(0)
+    slots = buf.shape[0]
     z, core = place[1], place[2]
 
-    def copies(b, slot):
+    def copies(b):
+        slot = lax.rem(b, slots)
         made = []
-        for c in range(2):
-            for i, (hop, start) in enumerate(hops):
-                piece = pieces[count * c + i].at[:, b]
-                at = lax.rem(z + hop, 4) * 2 + (core if c == 0 else 1 - core)
-                to = buf.at[slot, at, pl.ds(start, piece.shape[0])]
-                made.append(pltpu.make_async_copy(piece, to, sems.at[slot, count * c + i]))
-        return made
-
-    slot = lax.rem(step, 2)
+        if hops is None:
+            for i in range(buf.shape[1]):
+                made.append((refs[0].at[i, :, b], buf.at[slot, i]))
+        else:
+            for c in range(2):
+                for i, (hop, start) in enumerate(hops):
+                    piece = refs[len(hops) * c + i].at[:, b]
+                    at = lax.rem(z + hop, 4) * 2 + (core if c == 0 else 1 - core)
+                    made.append((piece, buf.at[slot, at, pl.ds(start, piece.shape[0])]))
+        return [
+            pltpu.make_async_copy(piece, to, sems.at[slot, i]) for i, (piece, to) in enumerate(made)
+        ]
 
     @pl.when(step == 0)
     def _():
-        for copy in copies(0, 0):
+        for copy in copies(0):
             copy.start()
 
-    @pl.when(step + 1 < pl.num_programs(0))
+    for ahead in range(1, slots - 1):
+
+        @pl.when((step == 0) & (ahead < steps))
+        def _():
+            for copy in copies(ahead):
+                copy.start()
+
+    @pl.when(step + slots - 1 < steps)
     def _():
-        for copy in copies(step + 1, 1 - slot):
+        for copy in copies(step + slots - 1):
             copy.start()
 
-    for copy in copies(step, slot):
+    for copy in copies(step):
         copy.wait()
 
+    slot = lax.rem(step, slots)
     segments = own.shape[0]
     columns = buf.shape[1] * buf.shape[3]
     right = [buf[slot, :, s].reshape(columns, LANES) for s in range(segments)]
@@ -197,30 +201,23 @@
     half = chan // 2
     bases = [] if base is None else [base]
     anywhere = pl.BlockSpec(memory_space=pl.ANY)
-    if isinstance(others, list):
-        kernel = functools.partial(pieces_kernel, 1.0 / window_count, hops)
-        specs = [anywhere] * len(others)
-        scratch = [
-            pltpu.VMEM((2, half, segments, rows, lanes), own.dtype),
-            pltpu.SemaphoreType.DMA((2, len(others))),
-        ]
-    else:
-        kernel = functools.partial(gathered_kernel, 1.0 / window_count)
-        specs = [pl.BlockSpec((half, segments, 1, rows, lanes), lambda b, at: (0, 0, b, 0, 0))]
+    if not isinstance(others, list):
         others = [others]
-        scratch = []
+    copies = half if hops is None else len(others)
     return pl.pallas_call(
-        kernel,
+        functools.partial(cross_kernel, 1.0 / window_count, hops),
         grid_spec=pltpu.PrefetchScalarGridSpec(
             num_scalar_prefetch=1,
             grid=(bins,),
             in_specs=[pl.BlockSpec((segments, 1, rows, lanes), lambda b, at: (0, b, 0, 0))]
-            + specs
-            + [anywhere] * len(bases),
+            + [anywhere] * (len(others) + len(bases)),
             out_specs=pl.BlockSpec(
                 (1, 2, rows, half * rows), lambda b, at: (b + first_bin, 0, 0, at[0])
             ),
-            scratch_shapes=scratch,
+            scratch_shapes=[
+                pltpu.VMEM((SLOTS, half, segments, rows, lanes), own.dtype),
+                pltpu.SemaphoreType.DMA((SLOTS, copies)),
+            ],
         ),
         out_shape=jax.ShapeDtypeStruct((all_bins, 2, rows, chan * rows), jnp.float32),
         input_output_aliases={2 + len(others): 0} if bases else {},
@@ -258,8 +255,9 @@
     return lax.all_to_all(value, "seg", split_axis=0, concat_axis=0, tiled=True)
 
 
-FIRST = 6
+FIRST = 5
 SPLIT = 4
+SLOTS = 3
 
 
 def local(strain_rate, window_starts):

time: 230 us -> 226 us (0.983)
  blocking collectives: 64.5 us -> 22.7 us
  waiting for transfers between devices: 53.4 us -> 91.2 us
  starting transfers between devices: 21.6 us -> 25.2 us
  local copies, waits for them, and re-layouts: 17.6 us -> 14.3 us
    all_to_all x2 -> x1, blocking collectives: 64.5 us -> 22.7 us  [exchange(): return lax.all_to_all(value, 'seg', split_axis=0, concat_axis=0, tiled=True)]
    ppermute x18, waiting for transfers between devices: 43.1 us -> 66.1 us  [send(): return lax.ppermute(value, 'chan', pairs)]
    all_to_all x0 -> x1, waiting for transfers between devices: none -> 17.8 us  [exchange(): return lax.all_to_all(value, 'seg', split_axis=0, concat_axis=0, tiled=True)]
    all_to_all x0 -> x1, starting transfers between devices: none -> 3.59 us  [exchange(): return lax.all_to_all(value, 'seg', split_axis=0, concat_axis=0, tiled=True)]
    unnamed x36 -> x34, local copies, waits for them, and re-layouts: 9.89 us -> 6.59 us
    all_gather x3, waiting for transfers between devices: 10.3 us -> 7.27 us  [gather(): return lax.all_gather(value, 'chan', axis_index_groups=X_HALVES)]
  transfers between devices with their start and end apart: 21 -> 22, of which waited for: 9 -> 9; matrix products, arithmetic and copies ran while one was open for 4% -> 4% of each run, Pallas kernels for 15% -> 14%
where the time goes in v5:
time: 226 us; the launch traced here: 225 us
  waiting for transfers between devices  91.2 us (40%)
  Pallas kernels  57 us (25%)
  starting transfers between devices  25.2 us (11%)
  blocking collectives  22.7 us (10%)
  local copies, waits for them, and re-layouts  14.3 us (6%)
  between operations  13.3 us (6%)
    ppermute x18, waiting for transfers between devices, send(): return lax.ppermute(value, 'chan', pairs)  66.1 us
    pallas_call x5, Pallas kernels, cross(): pl.pallas_call(functools.partial(cross_kernel, 1.0 / window_count, hops),...  42.1 us
    all_to_all x1, blocking collectives, exchange(): return lax.all_to_all(value, 'seg', split_axis=0, concat_axis=0, tiled=True)  22.7 us
    ppermute x18, starting transfers between devices, send(): return lax.ppermute(value, 'chan', pairs)  21.6 us
    all_to_all x1, waiting for transfers between devices, exchange(): return lax.all_to_all(value, 'seg', split_axis=0, concat_axis=0, tiled=True)  17.8 us
    pallas_call x1, Pallas kernels, local_spectra(): pl.pallas_call(spectra_kernel, grid=(channels // GROUP,), in_specs=[pl.Bl...  14.9 us
    all_gather x3, waiting for transfers between devices, gather(): return lax.all_gather(value, 'chan', axis_index_groups=X_HALVES)  7.27 us
    unnamed x34, local copies, waits for them, and re-layouts  6.59 us
  transfers between devices with their start and end apart: 22, of which 9 were waited for; matrix products, arithmetic and copies ran while one was open for 4% of the time, Pallas kernels for 14%

profile of v5, /device:TPU:1, one launch (start us, length us, event | category | flops | bytes accessed | tf_op | source)
XLA Modules:
  0.0 225.0 jit_solution(9874074850042649426)
XLA Ops:
  6.5 1.0 copy-done
  8.9 14.9 %spectra.1 = (bf16[8,5,96,128]{3,2,1,0:T(8,128)(2,1)S(1)}, bf16[8,7,96,128]{3,2,1,0:T(8,128)(2,1)}) custom-call(s32[64]{0:T(128)S(1)} %copy-done.2, bf16[96,33792]{1,0:T(8,128)(2,1)} %samples.1, bf16[1024,256]{1,0:T(8,128)(2,1)S(1)} %copy-done, f32[1,1024]{1,0:T(1,128)S(1)} %copy-done.1), custom_call_target="tpu_custom_call" | custom-call | tf_op jit(solution)/shard_map/spectra/pallas_call | solution.py:89
  23.8 22.7 %all_to_all.10.own = bf16[8,5,96,128]{3,2,1,0:T(8,128)(2,1)} all-to-all(bf16[8,5,96,128]{3,2,1,0:T(8,128)(2,1)S(1)} %get-tuple-element.14), channel_id=1, replica_groups=mesh['chan'=16,'seg'=8] {'seg'}, dimensions={0} | all-to-all | bytes 1966080 | tf_op jit(solution)/shard_map/all_to_all | solution.py:255
  46.5 3.6 %all-to-all-start = ((bf16[8,7,96,128]{3,2,1,0:T(8,128)(2,1)}), bf16[8,7,96,128]{3,2,1,0:T(8,128)(2,1)S(1)}, u32[]{:S(2)}, u32[]{:S(2)}) async-start(bf16[8,7,96,128]{3,2,1,0:T(8,128)(2,1)} %get-tuple-element.13), calls=%async_computation | async-start | bytes 2752512 | tf_op jit(solution)/shard_map/all_to_all | solution.py:255
  50.5 17.8 %all-to-all-done.refs_0_ = bf16[8,7,96,128]{3,2,1,0:T(8,128)(2,1)S(1)} async-done(((bf16[8,7,96,128]{3,2,1,0:T(8,128)(2,1)}), bf16[8,7,96,128]{3,2,1,0:T(8,128)(2,1)S(1)}, u32[]{:S(2)}, u32[]{:S(2)}) %all-to-all-start) | async-done | bytes 1376288 | tf_op jit(solution)/shard_map/all_to_all | solution.py:255
  68.3 17.0 %collective-permute-done.refs_1_.refs_0_ = bf16[8,5,96,128]{3,2,1,0:T(8,128)(2,1)S(1)} collective-permute-done((bf16[8,5,96,128]{3,2,1,0:T(8,128)(2,1)}, bf16[8,5,96,128]{3,2,1,0:T(8,128)(2,1)S(1)}, u32[]{:S(2)}, u32[]{:S(2)}) %collective-permute-start) | collective-permute-done | bytes 983072 | tf_op jit(solution)/shard_map/ppermute | solution.py:247
  85.3 1.0 copy-done.6
  86.3 2.1 slice.19.own
  88.5 1.2 collective-permute-start.1
  89.7 4.9 %all-gather.7.cloned.1.call-done = bf16[64,5,96,128]{3,2,1,0:T(8,128)(2,1)} async-done(((bf16[8,5,96,128]{3,2,1,0:T(8,128)(2,1)}), bf16[64,5,96,128]{3,2,1,0:T(8,128)(2,1)}) %all-gather.7.cloned.1.call-update) | async-done | bytes 7864336 | tf_op jit(solution)/shard_map/all_gather | solution.py:251
  94.6 3.4 %dynamic-slice_bitcast_fusion = (bf16[8,5,96,128]{3,2,1,0:T(8,128)(2,1)}, bf16[8,5,96,128]{3,2,1,0:T(8,128)(2,1)}, bf16[8,5,96,128]{3,2,1,0:T(8,128)(2,1)}) fusion(bf16[8,8,5,96,128]{4,3,2,1,0:T(8,128)(2,1)} %bitcast.13, s32[]{:T(128)S(6)} %select_n.23, s32[]{:T(128)S(6)} %select_n.22, s32[]{:T(128)S(6)} %select_n.21), kind=kLoop, calls=%fused_computation | loop fusion | bytes 5898252 | tf_op jit(solution)/shard_map/jit(dynamic_index_in_dim)/squeeze | solution.py:289
  98.0 19.8 %collective-permute-done.1.refs_0_ = bf16[8,7,96,128]{3,2,1,0:T(8,128)(2,1)S(1)} collective-permute-done((bf16[8,7,96,128]{3,2,1,0:T(8,128)(2,1)}, bf16[8,7,96,128]{3,2,1,0:T(8,128)(2,1)S(1)}, u32[]{:S(2)}, u32[]{:S(2)}) %collective-permute-start.1) | collective-permute-done | bytes 1376288 | tf_op jit(solution)/shard_map/ppermute | solution.py:247
  117.9 1.1 copy-done.4
  118.9 1.1 slice.16.own.refs_0_
  120.1 1.8 collective-permute-start.4
  121.9 2.1 collective-permute-start.5
  124.0 3.8 %collective-permute-start.8 = (bf16[8,3,96,128]{3,2,1,0:T(8,128)(2,1)S(1)}, bf16[8,3,96,128]{3,2,1,0:T(8,128)(2,1)S(1)}, u32[]{:S(2)}, u32[]{:S(2)}) collective-permute-start(bf16[8,3,96,128]{3,2,1,0:T(8,128)(2,1)S(1)} %slice.16.own.refs_0_), channel_id=1, source_target_pairs={{0,8},{8,0},{16,24},{24,16},{32,40},{40,32},{48,56},{56,48},{64,72... | collective-permute-start | bytes 1769480 | tf_op jit(solution)/shard_map/ppermute | solution.py:247
  127.8 1.1 collective-permute-start.2
  128.9 18.0 %collective-permute-done.4.refs_1_ = bf16[8,3,96,128]{3,2,1,0:T(8,128)(2,1)S(1)} collective-permute-done((bf16[8,3,96,128]{3,2,1,0:T(8,128)(2,1)S(1)}, bf16[8,3,96,128]{3,2,1,0:T(8,128)(2,1)S(1)}, u32[]{:S(2)}, u32[]{:S(2)}) %collective-permute-start.4) | collective-permute-done | bytes 589856 | tf_op jit(solution)/shard_map/ppermute | solution.py:247
  147.0 1.3 collective-permute-start.13
  149.6 2.7 %collective-permute-start.7 = (bf16[4,3,96,128]{3,2,1,0:T(8,128)(2,1)S(1)}, bf16[4,3,96,128]{3,2,1,0:T(8,128)(2,1)S(1)}, u32[]{:S(2)}, u32[]{:S(2)}) collective-permute-start(bf16[4,3,96,128]{3,2,1,0:T(8,128)(2,1)S(1)} %slice.18), channel_id=1, source_target_pairs={{0,48},{8,56},{16,0},{24,8},{32,16},{40,24},{48,32},{56,40},{64,11... | collective-permute-start | bytes 884744 | tf_op jit(solution)/shard_map/ppermute | solution.py:247
  152.2 2.9 %collective-permute-done.6.refs_3_ = bf16[4,3,96,128]{3,2,1,0:T(8,128)(2,1)S(1)} collective-permute-done((bf16[4,3,96,128]{3,2,1,0:T(8,128)(2,1)S(1)}, bf16[4,3,96,128]{3,2,1,0:T(8,128)(2,1)S(1)}, u32[]{:S(2)}, u32[]{:S(2)}) %collective-permute-start.6) | collective-permute-done | bytes 294944 | tf_op jit(solution)/shard_map/ppermute | solution.py:247
  155.1 2.6 %collective-permute-start.11 = (bf16[4,3,96,128]{3,2,1,0:T(8,128)(2,1)S(1)}, bf16[4,3,96,128]{3,2,1,0:T(8,128)(2,1)S(1)}, u32[]{:S(2)}, u32[]{:S(2)}) collective-permute-start(bf16[4,3,96,128]{3,2,1,0:T(8,128)(2,1)S(1)} %collective-permute-done.6.refs_3_), channel_id=1, source_target_pairs={{0,8},{8,0},{16,24},{24,16},{32,40},{40,32},{48,56},{56,48},{64,72... | collective-permute-start | bytes 884744 | tf_op jit(solution)/shard_map/ppermute | solution.py:247
  157.7 2.0 collective-permute-start.10
  162.0 8.5 %cross.5.refs_1_ = f32[12,2,96,1536]{3,2,1,0:T(8,128)} custom-call(s32[3]{0:T(128)} %after.6.place, bf16[8,5,96,128]{3,2,1,0:T(8,128)(2,1)} %all_to_all.10.own, bf16[8,8,5,96,128]{4,3,2,1,0:T(8,128)(2,1)} %bitcast.14), custom_call_target="tpu_custom_call" | custom-call | flops 1509949440 | bytes 10813440 | tf_op jit(solution)/shard_map/cross/pallas_call | solution.py:207
  170.7 7.7 %cross.6.refs_10_ = f32[12,2,96,1536]{3,2,1,0:T(8,128)} custom-call(s32[3]{0:T(128)} %after.6.place, bf16[8,4,96,128]{3,2,1,0:T(8,128)(2,1)} %slice.19.own, bf16[8,8,4,96,128]{4,3,2,1,0:T(8,128)(2,1)} %bitcast.16, f32[12,2,96,1536]{3,2,1,0:T(8,128)} %cross.5.refs_1_), custom_call_target="tpu_custom_call", output_to_operand_aliasing={{}: (3, {})} | custom-call | flops 1207959552 | bytes 8650752 | tf_op jit(solution)/shard_map/cross/pallas_call | solution.py:207
  178.6 6.8 %cross.7.refs_0_ = f32[12,2,96,1536]{3,2,1,0:T(8,128)} custom-call(s32[3]{0:T(128)} %after.6.place, bf16[8,3,96,128]{3,2,1,0:T(8,128)(2,1)} %copy-done.5, bf16[8,3,96,128]{3,2,1,0:T(8,128)(2,1)} %copy-done.5, bf16[8,3,96,128]{3,2,1,0:T(8,128)(2,1)} %copy-done.11, ...), custom_call_target="tpu_custom_call", output_to_operand_aliasing={{}: (12, {})} | custom-call | flops 905969664 | bytes 6488064 | tf_op jit(solution)/shard_map/cross/pallas_call | solution.py:207
  187.2 6.4 %collective-permute-done.3.refs_2_ = bf16[8,5,96,128]{3,2,1,0:T(8,128)(2,1)} collective-permute-done((bf16[8,5,96,128]{3,2,1,0:T(8,128)(2,1)}, bf16[8,5,96,128]{3,2,1,0:T(8,128)(2,1)}, u32[]{:S(2)}, u32[]{:S(2)}) %collective-permute-start.3) | collective-permute-done | bytes 983072 | tf_op jit(solution)/shard_map/ppermute | solution.py:247
  195.0 2.0 collective-permute-done.16.refs_6_
  197.0 8.6 %cross.8.refs_1_ = f32[12,2,96,1536]{3,2,1,0:T(8,128)} custom-call(s32[3]{0:T(128)} %add_add_fusion.place, bf16[8,5,96,128]{3,2,1,0:T(8,128)(2,1)} %all_to_all.10.own, bf16[8,5,96,128]{3,2,1,0:T(8,128)(2,1)} %copy-done.6, bf16[8,5,96,128]{3,2,1,0:T(8,128)(2,1)} %copy-done.8, ...), custom_call_target="tpu_custom_call", output_to_operand_aliasing={{}: (10, {})} | custom-call | flops 1509949440 | bytes 10813440 | tf_op jit(solution)/shard_map/cross/pallas_call | solution.py:207
  205.6 2.4 %all-gather.9.cloned.1.call-done = bf16[64,7,96,128]{3,2,1,0:T(8,128)(2,1)} async-done(((bf16[8,7,96,128]{3,2,1,0:T(8,128)(2,1)}), bf16[64,7,96,128]{3,2,1,0:T(8,128)(2,1)}) %all-gather.9.cloned.1.call-update) | async-done | bytes 11010064 | tf_op jit(solution)/shard_map/all_gather | solution.py:251
  208.0 10.5 %cross.9 = f32[12,2,96,1536]{3,2,1,0:T(8,128)} custom-call(s32[3]{0:T(128)} %add_add_fusion.place, bf16[8,7,96,128]{3,2,1,0:T(8,128)(2,1)} %after.4.own, bf16[8,8,7,96,128]{4,3,2,1,0:T(8,128)(2,1)} %bitcast.15, f32[12,2,96,1536]{3,2,1,0:T(8,128)} %cross.8.refs_1_), custom_call_target="tpu_custom_call", output_to_operand_aliasing={{}: (3, {})} | custom-call | flops 2113929216 | bytes 15138816 | tf_op jit(solution)/shard_map/cross/pallas_call | solution.py:207
  (67 shorter events, 9.1 us)
Async XLA Ops:
  6.5 88.0 %all-gather.7.cloned.1.call-start = ((), (), s32[]{:S(2)}) async-start(), calls=%async_computation.2 | async-start | bytes 8847360 | tf_op jit(solution)/shard_map/all_gather | solution.py:251
  46.5 21.8 %all-to-all-start = ((bf16[8,7,96,128]{3,2,1,0:T(8,128)(2,1)}), bf16[8,7,96,128]{3,2,1,0:T(8,128)(2,1)S(1)}, u32[]{:S(2)}, u32[]{:S(2)}) async-start(bf16[8,7,96,128]{3,2,1,0:T(8,128)(2,1)} %get-tuple-element.13), calls=%async_computation | async-start | bytes 2752512 | tf_op jit(solution)/shard_map/all_to_all | solution.py:255
  50.1 120.6 %all-gather.11.cloned.1.call-start = ((), (), s32[]{:S(2)}) async-start(), calls=%async_computation.4 | async-start | bytes 7077888 | tf_op jit(solution)/shard_map/all_gather | solution.py:251
  50.1 35.2 %collective-permute-start = (bf16[8,5,96,128]{3,2,1,0:T(8,128)(2,1)}, bf16[8,5,96,128]{3,2,1,0:T(8,128)(2,1)S(1)}, u32[]{:S(2)}, u32[]{:S(2)}) collective-permute-start(bf16[8,5,96,128]{3,2,1,0:T(8,128)(2,1)} %all_to_all.10.own), channel_id=1, source_target_pairs={{0,64},{8,72},{16,80},{24,88},{32,96},{40,104},{48,112},{56,120},{... | collective-permute-start | bytes 2949128 | tf_op jit(solution)/shard_map/ppermute | solution.py:247
  68.3 17.0 %copy-start.3 = (bf16[8,7,96,128]{3,2,1,0:T(8,128)(2,1)}, bf16[8,7,96,128]{3,2,1,0:T(8,128)(2,1)S(1)}, u32[]{:S(2)}) copy-start(bf16[8,7,96,128]{3,2,1,0:T(8,128)(2,1)S(1)} %all-to-all-done.refs_0_) | copy-start | bytes 4128772
  88.4 119.5 %all-gather.9.cloned.1.call-start = ((), (), s32[]{:S(2)}) async-start(), calls=%async_computation.3 | async-start | bytes 12386304 | tf_op jit(solution)/shard_map/all_gather | solution.py:251
  88.5 29.4 %collective-permute-start.1 = (bf16[8,7,96,128]{3,2,1,0:T(8,128)(2,1)}, bf16[8,7,96,128]{3,2,1,0:T(8,128)(2,1)S(1)}, u32[]{:S(2)}, u32[]{:S(2)}) collective-permute-start(bf16[8,7,96,128]{3,2,1,0:T(8,128)(2,1)} %after.4.own), channel_id=1, source_target_pairs={{0,64},{8,72},{16,80},{24,88},{32,96},{40,104},{48,112},{56,120},{... | collective-permute-start | bytes 4128776 | tf_op jit(solution)/shard_map/ppermute | solution.py:247
  117.9 1.1 copy-start.4
  120.1 50.5 %copy-start.5 = (bf16[8,3,96,128]{3,2,1,0:T(8,128)(2,1)}, bf16[8,3,96,128]{3,2,1,0:T(8,128)(2,1)S(1)}, u32[]{:S(2)}) copy-start(bf16[8,3,96,128]{3,2,1,0:T(8,128)(2,1)S(1)} %slice.16.own.refs_0_) | copy-start | bytes 1769476
  120.1 26.8 %collective-permute-start.4 = (bf16[8,3,96,128]{3,2,1,0:T(8,128)(2,1)S(1)}, bf16[8,3,96,128]{3,2,1,0:T(8,128)(2,1)S(1)}, u32[]{:S(2)}, u32[]{:S(2)}) collective-permute-start(bf16[8,3,96,128]{3,2,1,0:T(8,128)(2,1)S(1)} %slice.16.own.refs_0_), channel_id=1, source_target_pairs={{0,16},{8,24},{16,32},{24,40},{32,48},{40,56},{48,0},{56,8},{64,80... | collective-permute-start | bytes 1769480 | tf_op jit(solution)/shard_map/ppermute | solution.py:247
  121.9 26.4 %collective-permute-start.5 = (bf16[8,3,96,128]{3,2,1,0:T(8,128)(2,1)S(1)}, bf16[8,3,96,128]{3,2,1,0:T(8,128)(2,1)}, u32[]{:S(2)}, u32[]{:S(2)}) collective-permute-start(bf16[8,3,96,128]{3,2,1,0:T(8,128)(2,1)S(1)} %slice.16.own.refs_0_), channel_id=1, source_target_pairs={{0,48},{8,56},{16,0},{24,8},{32,16},{40,24},{48,32},{56,40},{64,11... | collective-permute-start | bytes 1769480 | tf_op jit(solution)/shard_map/ppermute | solution.py:247
  124.0 25.6 %collective-permute-start.8 = (bf16[8,3,96,128]{3,2,1,0:T(8,128)(2,1)S(1)}, bf16[8,3,96,128]{3,2,1,0:T(8,128)(2,1)S(1)}, u32[]{:S(2)}, u32[]{:S(2)}) collective-permute-start(bf16[8,3,96,128]{3,2,1,0:T(8,128)(2,1)S(1)} %slice.16.own.refs_0_), channel_id=1, source_target_pairs={{0,8},{8,0},{16,24},{24,16},{32,40},{40,32},{48,56},{56,48},{64,72... | collective-permute-start | bytes 1769480 | tf_op jit(solution)/shard_map/ppermute | solution.py:247
  127.8 33.3 %collective-permute-start.2 = (bf16[8,5,96,128]{3,2,1,0:T(8,128)(2,1)}, bf16[8,5,96,128]{3,2,1,0:T(8,128)(2,1)S(1)}, u32[]{:S(2)}, u32[]{:S(2)}) collective-permute-start(bf16[8,5,96,128]{3,2,1,0:T(8,128)(2,1)} %get-tuple-element.16), channel_id=1, source_target_pairs={{0,64},{8,72},{16,80},{24,88},{32,96},{40,104},{48,112},{56,120},{... | collective-permute-start | bytes 2949128 | tf_op jit(solution)/shard_map/ppermute | solution.py:247
  146.9 23.7 %copy-start.11 = (bf16[8,3,96,128]{3,2,1,0:T(8,128)(2,1)}, bf16[8,3,96,128]{3,2,1,0:T(8,128)(2,1)S(1)}, u32[]{:S(2)}) copy-start(bf16[8,3,96,128]{3,2,1,0:T(8,128)(2,1)S(1)} %collective-permute-done.4.refs_1_) | copy-start | bytes 1769476
  147.0 8.2 %collective-permute-start.6 = (bf16[4,3,96,128]{3,2,1,0:T(8,128)(2,1)S(1)}, bf16[4,3,96,128]{3,2,1,0:T(8,128)(2,1)S(1)}, u32[]{:S(2)}, u32[]{:S(2)}) collective-permute-start(bf16[4,3,96,128]{3,2,1,0:T(8,128)(2,1)S(1)} %slice.17), channel_id=1, source_target_pairs={{0,16},{8,24},{16,32},{24,40},{32,48},{40,56},{48,0},{56,8},{64,80... | collective-permute-start | bytes 884744 | tf_op jit(solution)/shard_map/ppermute | solution.py:247
  147.0 38.3 %collective-permute-start.13 = (bf16[8,5,96,128]{3,2,1,0:T(8,128)(2,1)}, bf16[8,5,96,128]{3,2,1,0:T(8,128)(2,1)S(1)}, u32[]{:S(2)}, u32[]{:S(2)}) collective-permute-start(bf16[8,5,96,128]{3,2,1,0:T(8,128)(2,1)} %get-tuple-element.18), channel_id=1, source_target_pairs={{0,64},{8,72},{16,80},{24,88},{32,96},{40,104},{48,112},{56,120},{... | collective-permute-start | bytes 2949128 | tf_op jit(solution)/shard_map/ppermute | solution.py:247
  148.3 45.3 %collective-permute-start.3 = (bf16[8,5,96,128]{3,2,1,0:T(8,128)(2,1)}, bf16[8,5,96,128]{3,2,1,0:T(8,128)(2,1)}, u32[]{:S(2)}, u32[]{:S(2)}) collective-permute-start(bf16[8,5,96,128]{3,2,1,0:T(8,128)(2,1)} %get-tuple-element.17), channel_id=1, source_target_pairs={{0,64},{8,72},{16,80},{24,88},{32,96},{40,104},{48,112},{56,120},{... | collective-permute-start | bytes 2949128 | tf_op jit(solution)/shard_map/ppermute | solution.py:247
  149.6 10.1 %copy-start.13 = (bf16[8,3,96,128]{3,2,1,0:T(8,128)(2,1)}, bf16[8,3,96,128]{3,2,1,0:T(8,128)(2,1)S(1)}, u32[]{:S(2)}) copy-start(bf16[8,3,96,128]{3,2,1,0:T(8,128)(2,1)S(1)} %collective-permute-done.8.refs_5_) | copy-start | bytes 1769476
  149.6 8.1 %collective-permute-start.7 = (bf16[4,3,96,128]{3,2,1,0:T(8,128)(2,1)S(1)}, bf16[4,3,96,128]{3,2,1,0:T(8,128)(2,1)S(1)}, u32[]{:S(2)}, u32[]{:S(2)}) collective-permute-start(bf16[4,3,96,128]{3,2,1,0:T(8,128)(2,1)S(1)} %slice.18), channel_id=1, source_target_pairs={{0,48},{8,56},{16,0},{24,8},{32,16},{40,24},{48,32},{56,40},{64,11... | collective-permute-start | bytes 884744 | tf_op jit(solution)/shard_map/ppermute | solution.py:247
  155.1 23.2 %copy-start.14 = (bf16[4,3,96,128]{3,2,1,0:T(8,128)(2,1)}, bf16[4,3,96,128]{3,2,1,0:T(8,128)(2,1)S(1)}, u32[]{:S(2)}) copy-start(bf16[4,3,96,128]{3,2,1,0:T(8,128)(2,1)S(1)} %collective-permute-done.6.refs_3_) | copy-start | bytes 884740
  155.1 4.6 %collective-permute-start.11 = (bf16[4,3,96,128]{3,2,1,0:T(8,128)(2,1)S(1)}, bf16[4,3,96,128]{3,2,1,0:T(8,128)(2,1)S(1)}, u32[]{:S(2)}, u32[]{:S(2)}) collective-permute-start(bf16[4,3,96,128]{3,2,1,0:T(8,128)(2,1)S(1)} %collective-permute-done.6.refs_3_), channel_id=1, source_target_pairs={{0,8},{8,0},{16,24},{24,16},{32,40},{40,32},{48,56},{56,48},{64,72... | collective-permute-start | bytes 884744 | tf_op jit(solution)/shard_map/ppermute | solution.py:247
  157.7 2.0 copy-start.15
  157.7 20.9 %collective-permute-start.10 = (bf16[8,3,96,128]{3,2,1,0:T(8,128)(2,1)}, bf16[8,3,96,128]{3,2,1,0:T(8,128)(2,1)}, u32[]{:S(2)}, u32[]{:S(2)}) collective-permute-start(bf16[8,3,96,128]{3,2,1,0:T(8,128)(2,1)} %collective-permute-done.5.refs_2_), channel_id=1, source_target_pairs={{0,8},{8,0},{16,24},{24,16},{32,40},{40,32},{48,56},{56,48},{64,72... | collective-permute-start | bytes 1769480 | tf_op jit(solution)/shard_map/ppermute | solution.py:247
  160.4 18.2 %collective-permute-start.9 = (bf16[8,3,96,128]{3,2,1,0:T(8,128)(2,1)S(1)}, bf16[8,3,96,128]{3,2,1,0:T(8,128)(2,1)}, u32[]{:S(2)}, u32[]{:S(2)}) collective-permute-start(bf16[8,3,96,128]{3,2,1,0:T(8,128)(2,1)S(1)} %collective-permute-done.4.refs_1_), channel_id=1, source_target_pairs={{0,8},{8,0},{16,24},{24,16},{32,40},{40,32},{48,56},{56,48},{64,72... | collective-permute-start | bytes 1769480 | tf_op jit(solution)/shard_map/ppermute | solution.py:247
  161.1 17.2 %collective-permute-start.12 = (bf16[4,3,96,128]{3,2,1,0:T(8,128)(2,1)}, bf16[4,3,96,128]{3,2,1,0:T(8,128)(2,1)}, u32[]{:S(2)}, u32[]{:S(2)}) collective-permute-start(bf16[4,3,96,128]{3,2,1,0:T(8,128)(2,1)} %copy-done.15), channel_id=1, source_target_pairs={{0,8},{8,0},{16,24},{24,16},{32,40},{40,32},{48,56},{56,48},{64,72... | collective-permute-start | bytes 884744 | tf_op jit(solution)/shard_map/ppermute | solution.py:247
  170.6 7.7 %copy-start.7 = (bf16[8,5,96,128]{3,2,1,0:T(8,128)(2,1)S(1)}, bf16[8,5,96,128]{3,2,1,0:T(8,128)(2,1)}, u32[]{:S(2)}) copy-start(bf16[8,5,96,128]{3,2,1,0:T(8,128)(2,1)} %copy-done.6) | copy-start | bytes 2949124
  178.3 16.6 %collective-permute-start.14 = (bf16[8,5,96,128]{3,2,1,0:T(8,128)(2,1)S(1)}, bf16[8,5,96,128]{3,2,1,0:T(8,128)(2,1)}, u32[]{:S(2)}, u32[]{:S(2)}) collective-permute-start(bf16[8,5,96,128]{3,2,1,0:T(8,128)(2,1)S(1)} %copy-done.7), channel_id=1, source_target_pairs={{0,8},{8,0},{16,24},{24,16},{32,40},{40,32},{48,56},{56,48},{64,72... | collective-permute-start | bytes 2949128 | tf_op jit(solution)/shard_map/ppermute | solution.py:247
  185.4 1.6 copy-start.9
  186.4 8.6 %collective-permute-start.17 = (bf16[8,5,96,128]{3,2,1,0:T(8,128)(2,1)}, bf16[8,5,96,128]{3,2,1,0:T(8,128)(2,1)S(1)}, u32[]{:S(2)}, u32[]{:S(2)}) collective-permute-start(bf16[8,5,96,128]{3,2,1,0:T(8,128)(2,1)} %get-tuple-element.19.refs_3_), channel_id=1, source_target_pairs={{0,8},{8,0},{16,24},{24,16},{32,40},{40,32},{48,56},{56,48},{64,72... | collective-permute-start | bytes 2949128 | tf_op jit(solution)/shard_map/ppermute | solution.py:247
  186.9 8.0 %collective-permute-start.15 = (bf16[8,5,96,128]{3,2,1,0:T(8,128)(2,1)S(1)}, bf16[8,5,96,128]{3,2,1,0:T(8,128)(2,1)}, u32[]{:S(2)}, u32[]{:S(2)}) collective-permute-start(bf16[8,5,96,128]{3,2,1,0:T(8,128)(2,1)S(1)} %copy-done.9), channel_id=1, source_target_pairs={{0,8},{8,0},{16,24},{24,16},{32,40},{40,32},{48,56},{56,48},{64,72... | collective-permute-start | bytes 2949128 | tf_op jit(solution)/shard_map/ppermute | solution.py:247
  193.6 3.3 %collective-permute-start.16 = (bf16[8,5,96,128]{3,2,1,0:T(8,128)(2,1)}, bf16[8,5,96,128]{3,2,1,0:T(8,128)(2,1)}, u32[]{:S(2)}, u32[]{:S(2)}) collective-permute-start(bf16[8,5,96,128]{3,2,1,0:T(8,128)(2,1)} %collective-permute-done.3.refs_2_), channel_id=1, source_target_pairs={{0,8},{8,0},{16,24},{24,16},{32,40},{40,32},{48,56},{56,48},{64,72... | collective-permute-start | bytes 2949128 | tf_op jit(solution)/shard_map/ppermute | solution.py:247
  195.0 2.0 copy-start.12
  (7 other events, 6.0 us)
Sparse Core Ops, SparseCore 0:
  46.6 47.9 all-gather.6
  96.3 50.4 all-gather.10
  148.5 59.4 all-gather.8

commit v6 on v5

--- a/solution.py
+++ b/solution.py
@@ -17,9 +17,9 @@
 EPSILON = 1e-06
 CLIP_LEVEL = 1.5
 LANES = 128
-GROUP = 32
+GROUP = 48
 BATCH = 16
-STRIDE = 40
+STRIDE = 56
 
 
 def fourier_columns():

time: 226 us -> 226 us (level)
  no operation moved by 1% of the time
where the time goes in v6:
time: 226 us; the launch traced here: 225 us
  waiting for transfers between devices  91.3 us (40%)
  Pallas kernels  56.8 us (25%)
  starting transfers between devices  25.1 us (11%)
  blocking collectives  22.7 us (10%)
  local copies, waits for them, and re-layouts  14.4 us (6%)
  between operations  13.3 us (6%)
    ppermute x18, waiting for transfers between devices, send(): return lax.ppermute(value, 'chan', pairs)  66.2 us
    pallas_call x5, Pallas kernels, cross(): pl.pallas_call(functools.partial(cross_kernel, 1.0 / window_count, hops),...  42.1 us
    all_to_all x1, blocking collectives, exchange(): return lax.all_to_all(value, 'seg', split_axis=0, concat_axis=0, tiled=True)  22.7 us
    ppermute x18, starting transfers between devices, send(): return lax.ppermute(value, 'chan', pairs)  21.5 us
    all_to_all x1, waiting for transfers between devices, exchange(): return lax.all_to_all(value, 'seg', split_axis=0, concat_axis=0, tiled=True)  17.7 us
    pallas_call x1, Pallas kernels, local_spectra(): pl.pallas_call(spectra_kernel, grid=(channels // GROUP,), in_specs=[pl.Bl...  14.8 us
    all_gather x3, waiting for transfers between devices, gather(): return lax.all_gather(value, 'chan', axis_index_groups=X_HALVES)  7.28 us
    unnamed x34, local copies, waits for them, and re-layouts  6.69 us
  transfers between devices with their start and end apart: 22, of which 9 were waited for; matrix products, arithmetic and copies ran while one was open for 4% of the time, Pallas kernels for 14%

profile of v6, /device:TPU:1, one launch (start us, length us, event | category | flops | bytes accessed | tf_op | source)
XLA Modules:
  0.0 224.9 jit_solution(15687819878778377899)
XLA Ops:
  6.5 1.0 copy-done
  8.9 14.8 %spectra.1 = (bf16[8,5,96,128]{3,2,1,0:T(8,128)(2,1)S(1)}, bf16[8,7,96,128]{3,2,1,0:T(8,128)(2,1)}) custom-call(s32[64]{0:T(128)S(1)} %copy-done.2, bf16[96,33792]{1,0:T(8,128)(2,1)} %samples.1, bf16[1024,256]{1,0:T(8,128)(2,1)S(1)} %copy-done, f32[1,1024]{1,0:T(1,128)S(1)} %copy-done.1), custom_call_target="tpu_custom_call" | custom-call | tf_op jit(solution)/shard_map/spectra/pallas_call | solution.py:89
  23.7 22.7 %all_to_all.10.own = bf16[8,5,96,128]{3,2,1,0:T(8,128)(2,1)} all-to-all(bf16[8,5,96,128]{3,2,1,0:T(8,128)(2,1)S(1)} %get-tuple-element.14), channel_id=1, replica_groups=mesh['chan'=16,'seg'=8] {'seg'}, dimensions={0} | all-to-all | bytes 1966080 | tf_op jit(solution)/shard_map/all_to_all | solution.py:255
  46.4 3.6 %all-to-all-start = ((bf16[8,7,96,128]{3,2,1,0:T(8,128)(2,1)}), bf16[8,7,96,128]{3,2,1,0:T(8,128)(2,1)S(1)}, u32[]{:S(2)}, u32[]{:S(2)}) async-start(bf16[8,7,96,128]{3,2,1,0:T(8,128)(2,1)} %get-tuple-element.13), calls=%async_computation | async-start | bytes 2752512 | tf_op jit(solution)/shard_map/all_to_all | solution.py:255
  50.4 17.7 %all-to-all-done.refs_0_ = bf16[8,7,96,128]{3,2,1,0:T(8,128)(2,1)S(1)} async-done(((bf16[8,7,96,128]{3,2,1,0:T(8,128)(2,1)}), bf16[8,7,96,128]{3,2,1,0:T(8,128)(2,1)S(1)}, u32[]{:S(2)}, u32[]{:S(2)}) %all-to-all-start) | async-done | bytes 1376288 | tf_op jit(solution)/shard_map/all_to_all | solution.py:255
  68.2 17.0 %collective-permute-done.refs_1_.refs_0_ = bf16[8,5,96,128]{3,2,1,0:T(8,128)(2,1)S(1)} collective-permute-done((bf16[8,5,96,128]{3,2,1,0:T(8,128)(2,1)}, bf16[8,5,96,128]{3,2,1,0:T(8,128)(2,1)S(1)}, u32[]{:S(2)}, u32[]{:S(2)}) %collective-permute-start) | collective-permute-done | bytes 983072 | tf_op jit(solution)/shard_map/ppermute | solution.py:247
  85.2 1.0 copy-done.6
  86.2 2.1 slice.19.own
  88.4 1.2 collective-permute-start.1
  89.6 4.9 %all-gather.7.cloned.1.call-done = bf16[64,5,96,128]{3,2,1,0:T(8,128)(2,1)} async-done(((bf16[8,5,96,128]{3,2,1,0:T(8,128)(2,1)}), bf16[64,5,96,128]{3,2,1,0:T(8,128)(2,1)}) %all-gather.7.cloned.1.call-update) | async-done | bytes 7864336 | tf_op jit(solution)/shard_map/all_gather | solution.py:251
  94.5 3.4 %dynamic-slice_bitcast_fusion = (bf16[8,5,96,128]{3,2,1,0:T(8,128)(2,1)}, bf16[8,5,96,128]{3,2,1,0:T(8,128)(2,1)}, bf16[8,5,96,128]{3,2,1,0:T(8,128)(2,1)}) fusion(bf16[8,8,5,96,128]{4,3,2,1,0:T(8,128)(2,1)} %bitcast.13, s32[]{:T(128)S(6)} %select_n.23, s32[]{:T(128)S(6)} %select_n.22, s32[]{:T(128)S(6)} %select_n.21), kind=kLoop, calls=%fused_computation | loop fusion | bytes 5898252 | tf_op jit(solution)/shard_map/jit(dynamic_index_in_dim)/squeeze | solution.py:289
  97.9 19.8 %collective-permute-done.1.refs_0_ = bf16[8,7,96,128]{3,2,1,0:T(8,128)(2,1)S(1)} collective-permute-done((bf16[8,7,96,128]{3,2,1,0:T(8,128)(2,1)}, bf16[8,7,96,128]{3,2,1,0:T(8,128)(2,1)S(1)}, u32[]{:S(2)}, u32[]{:S(2)}) %collective-permute-start.1) | collective-permute-done | bytes 1376288 | tf_op jit(solution)/shard_map/ppermute | solution.py:247
  117.8 1.1 copy-done.4
  118.9 1.1 slice.16.own.refs_0_
  120.0 1.7 collective-permute-start.4
  121.7 2.2 collective-permute-start.5
  123.9 3.8 %collective-permute-start.8 = (bf16[8,3,96,128]{3,2,1,0:T(8,128)(2,1)S(1)}, bf16[8,3,96,128]{3,2,1,0:T(8,128)(2,1)S(1)}, u32[]{:S(2)}, u32[]{:S(2)}) collective-permute-start(bf16[8,3,96,128]{3,2,1,0:T(8,128)(2,1)S(1)} %slice.16.own.refs_0_), channel_id=1, source_target_pairs={{0,8},{8,0},{16,24},{24,16},{32,40},{40,32},{48,56},{56,48},{64,72... | collective-permute-start | bytes 1769480 | tf_op jit(solution)/shard_map/ppermute | solution.py:247
  127.7 1.1 collective-permute-start.2
  128.8 18.0 %collective-permute-done.4.refs_1_ = bf16[8,3,96,128]{3,2,1,0:T(8,128)(2,1)S(1)} collective-permute-done((bf16[8,3,96,128]{3,2,1,0:T(8,128)(2,1)S(1)}, bf16[8,3,96,128]{3,2,1,0:T(8,128)(2,1)S(1)}, u32[]{:S(2)}, u32[]{:S(2)}) %collective-permute-start.4) | collective-permute-done | bytes 589856 | tf_op jit(solution)/shard_map/ppermute | solution.py:247
  146.9 1.3 collective-permute-start.13
  149.5 2.7 %collective-permute-start.7 = (bf16[4,3,96,128]{3,2,1,0:T(8,128)(2,1)S(1)}, bf16[4,3,96,128]{3,2,1,0:T(8,128)(2,1)S(1)}, u32[]{:S(2)}, u32[]{:S(2)}) collective-permute-start(bf16[4,3,96,128]{3,2,1,0:T(8,128)(2,1)S(1)} %slice.18), channel_id=1, source_target_pairs={{0,48},{8,56},{16,0},{24,8},{32,16},{40,24},{48,32},{56,40},{64,11... | collective-permute-start | bytes 884744 | tf_op jit(solution)/shard_map/ppermute | solution.py:247
  152.1 2.9 %collective-permute-done.6.refs_3_ = bf16[4,3,96,128]{3,2,1,0:T(8,128)(2,1)S(1)} collective-permute-done((bf16[4,3,96,128]{3,2,1,0:T(8,128)(2,1)S(1)}, bf16[4,3,96,128]{3,2,1,0:T(8,128)(2,1)S(1)}, u32[]{:S(2)}, u32[]{:S(2)}) %collective-permute-start.6) | collective-permute-done | bytes 294944 | tf_op jit(solution)/shard_map/ppermute | solution.py:247
  155.0 2.6 %collective-permute-start.11 = (bf16[4,3,96,128]{3,2,1,0:T(8,128)(2,1)S(1)}, bf16[4,3,96,128]{3,2,1,0:T(8,128)(2,1)S(1)}, u32[]{:S(2)}, u32[]{:S(2)}) collective-permute-start(bf16[4,3,96,128]{3,2,1,0:T(8,128)(2,1)S(1)} %collective-permute-done.6.refs_3_), channel_id=1, source_target_pairs={{0,8},{8,0},{16,24},{24,16},{32,40},{40,32},{48,56},{56,48},{64,72... | collective-permute-start | bytes 884744 | tf_op jit(solution)/shard_map/ppermute | solution.py:247
  157.6 2.0 collective-permute-start.10
  161.9 8.5 %cross.5.refs_1_ = f32[12,2,96,1536]{3,2,1,0:T(8,128)} custom-call(s32[3]{0:T(128)} %after.6.place, bf16[8,5,96,128]{3,2,1,0:T(8,128)(2,1)} %all_to_all.10.own, bf16[8,8,5,96,128]{4,3,2,1,0:T(8,128)(2,1)} %bitcast.14), custom_call_target="tpu_custom_call" | custom-call | flops 1509949440 | bytes 10813440 | tf_op jit(solution)/shard_map/cross/pallas_call | solution.py:207
  170.5 7.6 %cross.6.refs_10_ = f32[12,2,96,1536]{3,2,1,0:T(8,128)} custom-call(s32[3]{0:T(128)} %after.6.place, bf16[8,4,96,128]{3,2,1,0:T(8,128)(2,1)} %slice.19.own, bf16[8,8,4,96,128]{4,3,2,1,0:T(8,128)(2,1)} %bitcast.16, f32[12,2,96,1536]{3,2,1,0:T(8,128)} %cross.5.refs_1_), custom_call_target="tpu_custom_call", output_to_operand_aliasing={{}: (3, {})} | custom-call | flops 1207959552 | bytes 8650752 | tf_op jit(solution)/shard_map/cross/pallas_call | solution.py:207
  178.5 6.8 %cross.7.refs_0_ = f32[12,2,96,1536]{3,2,1,0:T(8,128)} custom-call(s32[3]{0:T(128)} %after.6.place, bf16[8,3,96,128]{3,2,1,0:T(8,128)(2,1)} %copy-done.5, bf16[8,3,96,128]{3,2,1,0:T(8,128)(2,1)} %copy-done.5, bf16[8,3,96,128]{3,2,1,0:T(8,128)(2,1)} %copy-done.11, ...), custom_call_target="tpu_custom_call", output_to_operand_aliasing={{}: (12, {})} | custom-call | flops 905969664 | bytes 6488064 | tf_op jit(solution)/shard_map/cross/pallas_call | solution.py:207
  187.1 6.5 %collective-permute-done.3.refs_2_ = bf16[8,5,96,128]{3,2,1,0:T(8,128)(2,1)} collective-permute-done((bf16[8,5,96,128]{3,2,1,0:T(8,128)(2,1)}, bf16[8,5,96,128]{3,2,1,0:T(8,128)(2,1)}, u32[]{:S(2)}, u32[]{:S(2)}) %collective-permute-start.3) | collective-permute-done | bytes 983072 | tf_op jit(solution)/shard_map/ppermute | solution.py:247
  194.9 2.0 collective-permute-done.16.refs_6_
  196.9 8.6 %cross.8.refs_1_ = f32[12,2,96,1536]{3,2,1,0:T(8,128)} custom-call(s32[3]{0:T(128)} %add_add_fusion.place, bf16[8,5,96,128]{3,2,1,0:T(8,128)(2,1)} %all_to_all.10.own, bf16[8,5,96,128]{3,2,1,0:T(8,128)(2,1)} %copy-done.6, bf16[8,5,96,128]{3,2,1,0:T(8,128)(2,1)} %copy-done.8, ...), custom_call_target="tpu_custom_call", output_to_operand_aliasing={{}: (10, {})} | custom-call | flops 1509949440 | bytes 10813440 | tf_op jit(solution)/shard_map/cross/pallas_call | solution.py:207
  205.5 2.4 %all-gather.9.cloned.1.call-done = bf16[64,7,96,128]{3,2,1,0:T(8,128)(2,1)} async-done(((bf16[8,7,96,128]{3,2,1,0:T(8,128)(2,1)}), bf16[64,7,96,128]{3,2,1,0:T(8,128)(2,1)}) %all-gather.9.cloned.1.call-update) | async-done | bytes 11010064 | tf_op jit(solution)/shard_map/all_gather | solution.py:251
  207.9 10.5 %cross.9 = f32[12,2,96,1536]{3,2,1,0:T(8,128)} custom-call(s32[3]{0:T(128)} %add_add_fusion.place, bf16[8,7,96,128]{3,2,1,0:T(8,128)(2,1)} %after.4.own, bf16[8,8,7,96,128]{4,3,2,1,0:T(8,128)(2,1)} %bitcast.15, f32[12,2,96,1536]{3,2,1,0:T(8,128)} %cross.8.refs_1_), custom_call_target="tpu_custom_call", output_to_operand_aliasing={{}: (3, {})} | custom-call | flops 2113929216 | bytes 15138816 | tf_op jit(solution)/shard_map/cross/pallas_call | solution.py:207
  (67 shorter events, 9.1 us)
Async XLA Ops:
  6.5 87.9 %all-gather.7.cloned.1.call-start = ((), (), s32[]{:S(2)}) async-start(), calls=%async_computation.2 | async-start | bytes 8847360 | tf_op jit(solution)/shard_map/all_gather | solution.py:251
  46.4 21.8 %all-to-all-start = ((bf16[8,7,96,128]{3,2,1,0:T(8,128)(2,1)}), bf16[8,7,96,128]{3,2,1,0:T(8,128)(2,1)S(1)}, u32[]{:S(2)}, u32[]{:S(2)}) async-start(bf16[8,7,96,128]{3,2,1,0:T(8,128)(2,1)} %get-tuple-element.13), calls=%async_computation | async-start | bytes 2752512 | tf_op jit(solution)/shard_map/all_to_all | solution.py:255
  50.0 120.5 %all-gather.11.cloned.1.call-start = ((), (), s32[]{:S(2)}) async-start(), calls=%async_computation.4 | async-start | bytes 7077888 | tf_op jit(solution)/shard_map/all_gather | solution.py:251
  50.0 35.2 %collective-permute-start = (bf16[8,5,96,128]{3,2,1,0:T(8,128)(2,1)}, bf16[8,5,96,128]{3,2,1,0:T(8,128)(2,1)S(1)}, u32[]{:S(2)}, u32[]{:S(2)}) collective-permute-start(bf16[8,5,96,128]{3,2,1,0:T(8,128)(2,1)} %all_to_all.10.own), channel_id=1, source_target_pairs={{0,64},{8,72},{16,80},{24,88},{32,96},{40,104},{48,112},{56,120},{... | collective-permute-start | bytes 2949128 | tf_op jit(solution)/shard_map/ppermute | solution.py:247
  68.2 17.0 %copy-start.3 = (bf16[8,7,96,128]{3,2,1,0:T(8,128)(2,1)}, bf16[8,7,96,128]{3,2,1,0:T(8,128)(2,1)S(1)}, u32[]{:S(2)}) copy-start(bf16[8,7,96,128]{3,2,1,0:T(8,128)(2,1)S(1)} %all-to-all-done.refs_0_) | copy-start | bytes 4128772
  88.3 119.5 %all-gather.9.cloned.1.call-start = ((), (), s32[]{:S(2)}) async-start(), calls=%async_computation.3 | async-start | bytes 12386304 | tf_op jit(solution)/shard_map/all_gather | solution.py:251
  88.4 29.4 %collective-permute-start.1 = (bf16[8,7,96,128]{3,2,1,0:T(8,128)(2,1)}, bf16[8,7,96,128]{3,2,1,0:T(8,128)(2,1)S(1)}, u32[]{:S(2)}, u32[]{:S(2)}) collective-permute-start(bf16[8,7,96,128]{3,2,1,0:T(8,128)(2,1)} %after.4.own), channel_id=1, source_target_pairs={{0,64},{8,72},{16,80},{24,88},{32,96},{40,104},{48,112},{56,120},{... | collective-permute-start | bytes 4128776 | tf_op jit(solution)/shard_map/ppermute | solution.py:247
  117.8 1.1 copy-start.4
  120.0 50.5 %copy-start.5 = (bf16[8,3,96,128]{3,2,1,0:T(8,128)(2,1)}, bf16[8,3,96,128]{3,2,1,0:T(8,128)(2,1)S(1)}, u32[]{:S(2)}) copy-start(bf16[8,3,96,128]{3,2,1,0:T(8,128)(2,1)S(1)} %slice.16.own.refs_0_) | copy-start | bytes 1769476
  120.0 26.8 %collective-permute-start.4 = (bf16[8,3,96,128]{3,2,1,0:T(8,128)(2,1)S(1)}, bf16[8,3,96,128]{3,2,1,0:T(8,128)(2,1)S(1)}, u32[]{:S(2)}, u32[]{:S(2)}) collective-permute-start(bf16[8,3,96,128]{3,2,1,0:T(8,128)(2,1)S(1)} %slice.16.own.refs_0_), channel_id=1, source_target_pairs={{0,16},{8,24},{16,32},{24,40},{32,48},{40,56},{48,0},{56,8},{64,80... | collective-permute-start | bytes 1769480 | tf_op jit(solution)/shard_map/ppermute | solution.py:247
  121.7 26.5 %collective-permute-start.5 = (bf16[8,3,96,128]{3,2,1,0:T(8,128)(2,1)S(1)}, bf16[8,3,96,128]{3,2,1,0:T(8,128)(2,1)}, u32[]{:S(2)}, u32[]{:S(2)}) collective-permute-start(bf16[8,3,96,128]{3,2,1,0:T(8,128)(2,1)S(1)} %slice.16.own.refs_0_), channel_id=1, source_target_pairs={{0,48},{8,56},{16,0},{24,8},{32,16},{40,24},{48,32},{56,40},{64,11... | collective-permute-start | bytes 1769480 | tf_op jit(solution)/shard_map/ppermute | solution.py:247
  123.9 25.6 %collective-permute-start.8 = (bf16[8,3,96,128]{3,2,1,0:T(8,128)(2,1)S(1)}, bf16[8,3,96,128]{3,2,1,0:T(8,128)(2,1)S(1)}, u32[]{:S(2)}, u32[]{:S(2)}) collective-permute-start(bf16[8,3,96,128]{3,2,1,0:T(8,128)(2,1)S(1)} %slice.16.own.refs_0_), channel_id=1, source_target_pairs={{0,8},{8,0},{16,24},{24,16},{32,40},{40,32},{48,56},{56,48},{64,72... | collective-permute-start | bytes 1769480 | tf_op jit(solution)/shard_map/ppermute | solution.py:247
  127.7 33.3 %collective-permute-start.2 = (bf16[8,5,96,128]{3,2,1,0:T(8,128)(2,1)}, bf16[8,5,96,128]{3,2,1,0:T(8,128)(2,1)S(1)}, u32[]{:S(2)}, u32[]{:S(2)}) collective-permute-start(bf16[8,5,96,128]{3,2,1,0:T(8,128)(2,1)} %get-tuple-element.16), channel_id=1, source_target_pairs={{0,64},{8,72},{16,80},{24,88},{32,96},{40,104},{48,112},{56,120},{... | collective-permute-start | bytes 2949128 | tf_op jit(solution)/shard_map/ppermute | solution.py:247
  146.8 23.6 %copy-start.11 = (bf16[8,3,96,128]{3,2,1,0:T(8,128)(2,1)}, bf16[8,3,96,128]{3,2,1,0:T(8,128)(2,1)S(1)}, u32[]{:S(2)}) copy-start(bf16[8,3,96,128]{3,2,1,0:T(8,128)(2,1)S(1)} %collective-permute-done.4.refs_1_) | copy-start | bytes 1769476
  146.9 8.2 %collective-permute-start.6 = (bf16[4,3,96,128]{3,2,1,0:T(8,128)(2,1)S(1)}, bf16[4,3,96,128]{3,2,1,0:T(8,128)(2,1)S(1)}, u32[]{:S(2)}, u32[]{:S(2)}) collective-permute-start(bf16[4,3,96,128]{3,2,1,0:T(8,128)(2,1)S(1)} %slice.17), channel_id=1, source_target_pairs={{0,16},{8,24},{16,32},{24,40},{32,48},{40,56},{48,0},{56,8},{64,80... | collective-permute-start | bytes 884744 | tf_op jit(solution)/shard_map/ppermute | solution.py:247
  146.9 38.4 %collective-permute-start.13 = (bf16[8,5,96,128]{3,2,1,0:T(8,128)(2,1)}, bf16[8,5,96,128]{3,2,1,0:T(8,128)(2,1)S(1)}, u32[]{:S(2)}, u32[]{:S(2)}) collective-permute-start(bf16[8,5,96,128]{3,2,1,0:T(8,128)(2,1)} %get-tuple-element.18), channel_id=1, source_target_pairs={{0,64},{8,72},{16,80},{24,88},{32,96},{40,104},{48,112},{56,120},{... | collective-permute-start | bytes 2949128 | tf_op jit(solution)/shard_map/ppermute | solution.py:247
  148.2 45.3 %collective-permute-start.3 = (bf16[8,5,96,128]{3,2,1,0:T(8,128)(2,1)}, bf16[8,5,96,128]{3,2,1,0:T(8,128)(2,1)}, u32[]{:S(2)}, u32[]{:S(2)}) collective-permute-start(bf16[8,5,96,128]{3,2,1,0:T(8,128)(2,1)} %get-tuple-element.17), channel_id=1, source_target_pairs={{0,64},{8,72},{16,80},{24,88},{32,96},{40,104},{48,112},{56,120},{... | collective-permute-start | bytes 2949128 | tf_op jit(solution)/shard_map/ppermute | solution.py:247
  149.5 10.1 %copy-start.13 = (bf16[8,3,96,128]{3,2,1,0:T(8,128)(2,1)}, bf16[8,3,96,128]{3,2,1,0:T(8,128)(2,1)S(1)}, u32[]{:S(2)}) copy-start(bf16[8,3,96,128]{3,2,1,0:T(8,128)(2,1)S(1)} %collective-permute-done.8.refs_5_) | copy-start | bytes 1769476
  149.5 8.1 %collective-permute-start.7 = (bf16[4,3,96,128]{3,2,1,0:T(8,128)(2,1)S(1)}, bf16[4,3,96,128]{3,2,1,0:T(8,128)(2,1)S(1)}, u32[]{:S(2)}, u32[]{:S(2)}) collective-permute-start(bf16[4,3,96,128]{3,2,1,0:T(8,128)(2,1)S(1)} %slice.18), channel_id=1, source_target_pairs={{0,48},{8,56},{16,0},{24,8},{32,16},{40,24},{48,32},{56,40},{64,11... | collective-permute-start | bytes 884744 | tf_op jit(solution)/shard_map/ppermute | solution.py:247
  155.0 23.1 %copy-start.14 = (bf16[4,3,96,128]{3,2,1,0:T(8,128)(2,1)}, bf16[4,3,96,128]{3,2,1,0:T(8,128)(2,1)S(1)}, u32[]{:S(2)}) copy-start(bf16[4,3,96,128]{3,2,1,0:T(8,128)(2,1)S(1)} %collective-permute-done.6.refs_3_) | copy-start | bytes 884740
  155.0 4.6 %collective-permute-start.11 = (bf16[4,3,96,128]{3,2,1,0:T(8,128)(2,1)S(1)}, bf16[4,3,96,128]{3,2,1,0:T(8,128)(2,1)S(1)}, u32[]{:S(2)}, u32[]{:S(2)}) collective-permute-start(bf16[4,3,96,128]{3,2,1,0:T(8,128)(2,1)S(1)} %collective-permute-done.6.refs_3_), channel_id=1, source_target_pairs={{0,8},{8,0},{16,24},{24,16},{32,40},{40,32},{48,56},{56,48},{64,72... | collective-permute-start | bytes 884744 | tf_op jit(solution)/shard_map/ppermute | solution.py:247
  157.6 2.0 copy-start.15
  157.6 20.9 %collective-permute-start.10 = (bf16[8,3,96,128]{3,2,1,0:T(8,128)(2,1)}, bf16[8,3,96,128]{3,2,1,0:T(8,128)(2,1)}, u32[]{:S(2)}, u32[]{:S(2)}) collective-permute-start(bf16[8,3,96,128]{3,2,1,0:T(8,128)(2,1)} %collective-permute-done.5.refs_2_), channel_id=1, source_target_pairs={{0,8},{8,0},{16,24},{24,16},{32,40},{40,32},{48,56},{56,48},{64,72... | collective-permute-start | bytes 1769480 | tf_op jit(solution)/shard_map/ppermute | solution.py:247
  160.3 18.2 %collective-permute-start.9 = (bf16[8,3,96,128]{3,2,1,0:T(8,128)(2,1)S(1)}, bf16[8,3,96,128]{3,2,1,0:T(8,128)(2,1)}, u32[]{:S(2)}, u32[]{:S(2)}) collective-permute-start(bf16[8,3,96,128]{3,2,1,0:T(8,128)(2,1)S(1)} %collective-permute-done.4.refs_1_), channel_id=1, source_target_pairs={{0,8},{8,0},{16,24},{24,16},{32,40},{40,32},{48,56},{56,48},{64,72... | collective-permute-start | bytes 1769480 | tf_op jit(solution)/shard_map/ppermute | solution.py:247
  161.0 17.2 %collective-permute-start.12 = (bf16[4,3,96,128]{3,2,1,0:T(8,128)(2,1)}, bf16[4,3,96,128]{3,2,1,0:T(8,128)(2,1)}, u32[]{:S(2)}, u32[]{:S(2)}) collective-permute-start(bf16[4,3,96,128]{3,2,1,0:T(8,128)(2,1)} %copy-done.15), channel_id=1, source_target_pairs={{0,8},{8,0},{16,24},{24,16},{32,40},{40,32},{48,56},{56,48},{64,72... | collective-permute-start | bytes 884744 | tf_op jit(solution)/shard_map/ppermute | solution.py:247
  170.5 7.7 %copy-start.7 = (bf16[8,5,96,128]{3,2,1,0:T(8,128)(2,1)S(1)}, bf16[8,5,96,128]{3,2,1,0:T(8,128)(2,1)}, u32[]{:S(2)}) copy-start(bf16[8,5,96,128]{3,2,1,0:T(8,128)(2,1)} %copy-done.6) | copy-start | bytes 2949124
  178.2 16.7 %collective-permute-start.14 = (bf16[8,5,96,128]{3,2,1,0:T(8,128)(2,1)S(1)}, bf16[8,5,96,128]{3,2,1,0:T(8,128)(2,1)}, u32[]{:S(2)}, u32[]{:S(2)}) collective-permute-start(bf16[8,5,96,128]{3,2,1,0:T(8,128)(2,1)S(1)} %copy-done.7), channel_id=1, source_target_pairs={{0,8},{8,0},{16,24},{24,16},{32,40},{40,32},{48,56},{56,48},{64,72... | collective-permute-start | bytes 2949128 | tf_op jit(solution)/shard_map/ppermute | solution.py:247
  185.3 1.6 copy-start.9
  186.3 8.6 %collective-permute-start.17 = (bf16[8,5,96,128]{3,2,1,0:T(8,128)(2,1)}, bf16[8,5,96,128]{3,2,1,0:T(8,128)(2,1)S(1)}, u32[]{:S(2)}, u32[]{:S(2)}) collective-permute-start(bf16[8,5,96,128]{3,2,1,0:T(8,128)(2,1)} %get-tuple-element.19.refs_3_), channel_id=1, source_target_pairs={{0,8},{8,0},{16,24},{24,16},{32,40},{40,32},{48,56},{56,48},{64,72... | collective-permute-start | bytes 2949128 | tf_op jit(solution)/shard_map/ppermute | solution.py:247
  186.9 8.0 %collective-permute-start.15 = (bf16[8,5,96,128]{3,2,1,0:T(8,128)(2,1)S(1)}, bf16[8,5,96,128]{3,2,1,0:T(8,128)(2,1)}, u32[]{:S(2)}, u32[]{:S(2)}) collective-permute-start(bf16[8,5,96,128]{3,2,1,0:T(8,128)(2,1)S(1)} %copy-done.9), channel_id=1, source_target_pairs={{0,8},{8,0},{16,24},{24,16},{32,40},{40,32},{48,56},{56,48},{64,72... | collective-permute-start | bytes 2949128 | tf_op jit(solution)/shard_map/ppermute | solution.py:247
  193.5 3.3 %collective-permute-start.16 = (bf16[8,5,96,128]{3,2,1,0:T(8,128)(2,1)}, bf16[8,5,96,128]{3,2,1,0:T(8,128)(2,1)}, u32[]{:S(2)}, u32[]{:S(2)}) collective-permute-start(bf16[8,5,96,128]{3,2,1,0:T(8,128)(2,1)} %collective-permute-done.3.refs_2_), channel_id=1, source_target_pairs={{0,8},{8,0},{16,24},{24,16},{32,40},{40,32},{48,56},{56,48},{64,72... | collective-permute-start | bytes 2949128 | tf_op jit(solution)/shard_map/ppermute | solution.py:247
  194.9 2.0 copy-start.12
  (7 other events, 6.0 us)
Sparse Core Ops, SparseCore 0:
  46.5 47.9 all-gather.6
  96.2 50.4 all-gather.10
  148.4 59.4 all-gather.8
